TPU v7x, 128 devices: a whole 4x4x4 slice. The times are simulated.
128 devices in a mesh: wave: 16 (over y, z), lev: 8 (over x, core).
Axes of the slice: x: 4, y: 4, z: 4, core: 2. Of those that a mesh axis runs over, the one named last changes fastest.
Arguments:
- spectral: bfloat16 [1280, 512, 1280], P('wave', 'lev'), may hold values from -6 to 6
- legendre: bfloat16 [1280, 128, 1280], P('wave'), may hold values from -0.0034179688 to 0.0034179688
- wave_map: int32 [1280], replicated, may hold values from 0 to 1279, each once
- row_points: int32 [128], replicated, may hold values from 20 to 5136, as said below
- brackets: int32 [8], replicated, may hold values from 0 to 30, as said below
- lev_weight: float32 [8], replicated, may hold values from 0.05 to 0.95
- climatology: float32 [8, 256, 5248], P('lev', 'wave'), may hold values from 0.1 to 1
Outputs:
- anomaly: float32 [8, 256, 5248], P('lev', 'wave')
Inputs may be any that keep to these rules, and one draw needn't show every extreme that they name: `wave_map`: each wavenumber once. `row_points`: each is 20 + 4 i for a whole number i below 1280; some row has 5136 points. `brackets`: pressure level p has its lower bracket level among the 4 model levels of band p (levels b * 4 to b * 4 + 3 for band b); some pressure level outside the last band takes the last level of its band; the last pressure level takes 32 - 2.
All inputs are finite; a program needn't handle non-finite values.
Results may differ from a plain program's by a relative error of at most 0.0003.
Values sent between devices are 32-bit elements; how exact they have to be, the bound alone decides.
A program may use at most 256 MiB of HBM per device.

v0:
```python
import math

import jax
import jax.numpy as jnp
from jax import lax
from jax.sharding import PartitionSpec as P

M = 1280
NT = 1280
LEV_DEV = 4
STEPS = 4
FIELDS = 2
ROWPAD = 5248


TWO_PI = 2.0 * math.pi


def synthesize(coeffs, wave_map, points):
    places = jnp.arange(ROWPAD, dtype=jnp.int32)
    fine_ids = jnp.arange(64, dtype=jnp.int32)
    coarse_ids = jnp.arange(M // 64, dtype=jnp.int32) * 64
    step_rad = TWO_PI / points.astype(jnp.float32)
    fine_angle = (fine_ids[:, None] * places[None, :] % points).astype(jnp.float32) * step_rad
    coarse_angle = (coarse_ids[:, None] * places[None, :] % points).astype(jnp.float32) * step_rad
    fine_cos = jnp.cos(fine_angle)[None, :, :]
    fine_sin = jnp.sin(fine_angle)[None, :, :]
    coarse_cos = jnp.cos(coarse_angle)[:, None, :]
    coarse_sin = jnp.sin(coarse_angle)[:, None, :]
    cosine = (coarse_cos * fine_cos - coarse_sin * fine_sin).reshape(M, ROWPAD)
    sine_part = (coarse_sin * fine_cos + coarse_cos * fine_sin).reshape(M, ROWPAD)
    orders = jnp.arange(M, dtype=jnp.int32)
    factor = jnp.where(orders == 0, 1.0, 2.0).astype(jnp.float32)
    factor = jnp.where(orders <= (points - 1) // 2, factor, 0.0)
    ordered = jnp.zeros_like(coeffs).at[wave_map].set(coeffs) * factor[:, None, None]
    real_part = lax.dot_general(
        ordered[:, :, 0],
        cosine,
        (((0,), (0,)), ((), ())),
        precision=lax.Precision.HIGHEST,
        preferred_element_type=jnp.float32,
    )
    imag_part = lax.dot_general(
        ordered[:, :, 1],
        sine_part,
        (((0,), (0,)), ((), ())),
        precision=lax.Precision.HIGHEST,
        preferred_element_type=jnp.float32,
    )
    return jnp.where(places[None, :] < points, real_part - imag_part, 0.0)


def kinetic(values):
    return 0.5 * jnp.mean(values[:, 0] * values[:, 0] + values[:, 1] * values[:, 1], axis=1)


def mixing_table(brackets, lev_weight, levels_all):
    level_ids = jnp.arange(levels_all, dtype=jnp.int32)
    lower_hit = (level_ids[None, :] == brackets[:, None]).astype(jnp.float32)
    upper_hit = (level_ids[None, :] == brackets[:, None] + 1).astype(jnp.float32)
    return lev_weight[:, None] * lower_hit + (1.0 - lev_weight[:, None]) * upper_hit


def local(spectral, legendre, wave_map, row_points, brackets, lev_weight, climatology):
    slot_count = spectral.shape[0]
    half_rows = legendre.shape[1]
    lat_total = 2 * half_rows
    wave_idx = lax.axis_index("wave")
    lev_idx = lax.axis_index("lev")
    wave_count = lax.axis_size("wave")
    lev_count = lax.axis_size("lev")
    band_rows = lat_total // wave_count
    levels_all = LEV_DEV * lev_count
    plev_all = brackets.shape[0]
    width_q = FIELDS * STEPS * 2
    mixing = mixing_table(brackets, lev_weight, levels_all)
    points_all = jnp.concatenate([row_points, row_points])
    own_waves = lax.dynamic_slice_in_dim(wave_map, wave_idx * slot_count, slot_count, 0)
    degree = jnp.arange(NT, dtype=jnp.int32)
    kept_mask = degree[None, :] >= own_waves[:, None]
    parity = (1 - 2 * ((degree[None, :] + own_waves[:, None]) % 2)).astype(jnp.bfloat16)
    plain_coeffs = jnp.where(kept_mask[:, None, :], spectral, jnp.zeros((), jnp.bfloat16))
    signed = plain_coeffs * parity[:, None, :]
    north_part = jnp.einsum(
        "scn,sjn->scj", plain_coeffs, legendre, preferred_element_type=jnp.float32
    )
    south_part = jnp.einsum("scn,sjn->scj", signed, legendre, preferred_element_type=jnp.float32)
    fourier = jnp.concatenate([north_part, south_part], axis=2)
    moved_coeffs = lax.all_to_all(
        lax.all_to_all(fourier, "wave", split_axis=2, concat_axis=0, tiled=True),
        "lev",
        split_axis=2,
        concat_axis=1,
        tiled=True,
    )
    rows_here = moved_coeffs.shape[2]
    first_row = wave_idx * band_rows + lev_idx * rows_here

    def grid_row(row_input):
        row_coeffs, points = row_input
        split_cols = row_coeffs.reshape(M, levels_all, width_q)
        mixed_cols = jnp.einsum("pl,mlq->mpq", mixing, split_cols, precision=lax.Precision.HIGHEST)
        values = synthesize(mixed_cols.reshape(M, plev_all * FIELDS * STEPS, 2), wave_map, points)
        values = values.reshape(plev_all, FIELDS, STEPS, ROWPAD)
        return kinetic(values)

    row_points_here = lax.dynamic_slice_in_dim(points_all, first_row, rows_here, 0)
    energy_rows = lax.map(grid_row, (jnp.moveaxis(moved_coeffs, 2, 0), row_points_here))
    energy_rows = jnp.transpose(energy_rows, (1, 0, 2))
    result = lax.all_to_all(energy_rows, "lev", split_axis=0, concat_axis=1, tiled=True)
    out_points = lax.dynamic_slice_in_dim(points_all, wave_idx * band_rows, band_rows, 0)
    places = jnp.arange(ROWPAD, dtype=jnp.int32)
    inside = places[None, None, :] < out_points[None, :, None]
    return jnp.where(inside, result - climatology, 0.0)


def solution(mesh):
    placed = (
        P("wave", "lev", None),
        P("wave", None, None),
        P(),
        P(),
        P(),
        P(),
        P("lev", "wave", None),
    )
    return jax.shard_map(
        local, mesh=mesh, in_specs=placed, out_specs=P("lev", "wave", None), check_vma=False
    )
```

profile of v0, /device:TPU:1, one launch (start us, length us, event | category | flops | bytes accessed | tf_op | source)
XLA Modules:
  0.0 532.9 jit_solution(17098561680177363108)
XLA Ops:
  0.0 0.8 dynamic_slice.27
  1.2 15.9 %fusion.39 = f32[80,64,128]{2,1,0:T(8,128)S(1)} fusion(bf16[80,128,1280]{2,1,0:T(8,128)(2,1)} %param.10, bf16[80,64,1280]{2,1,0:T(8,128)(2,1)} %param.9, pred[80,1280]{1,0:T(8,128)(4,1)S(1)} %iota_compare_fusion.7), kind=kOutput, calls=%fused_computation.58 | convolution fusion | flops 1684275200 | bytes 42045440 | tf_op jit(solution)/shard_map/scn,sjn->scj/dot_general | solution.py:84
  17.1 17.5 %fusion.37 = f32[80,64,128]{2,1,0:T(8,128)} fusion(bf16[80,128,1280]{2,1,0:T(8,128)(2,1)} %param.10, bf16[80,64,1280]{2,1,0:T(8,128)(2,1)} %param.9, pred[80,1280]{1,0:T(8,128)(4,1)S(1)} %iota_compare_fusion.7, bf16[80,1280]{1,0:T(8,128)(2,1)S(1)} %fusion.46), kind=kOutput, calls=%fused_computation.55 | convolution fusion | flops 1690828800 | bytes 42250240 | tf_op jit(solution)/shard_map/scn,sjn->scj/dot_general | solution.py:87
  34.7 4.6 pad_maximum_fusion
  39.2 8.1 %copy.29 = f32[80,64,256]{0,1,2:T(8,128)} copy(f32[80,64,256]{2,1,0:T(8,128)} %pad_maximum_fusion) | data formatting | bytes 10485760 | tf_op jit(solution)/shard_map/concatenate | solution.py:88
  47.3 103.5 %all_to_all.48 = f32[80,64,256]{0,1,2:T(8,128)S(1)} all-to-all(f32[80,64,256]{0,1,2:T(8,128)} %copy.29), channel_id=1, replica_groups=mesh['wave'=16,'lev'=8] {'wave'}, dimensions={2} | all-to-all | bytes 10485760 | tf_op jit(solution)/shard_map/all_to_all | solution.py:90
  150.8 9.8 %copy.36 = f32[16,80,64,16]{1,0,2,3:T(8,128)} copy(f32[16,80,64,16]{1,2,3,0:T(8,128)S(1)} %bitcast.67) | data formatting | bytes 10485760 | tf_op jit(solution)/shard_map/all_to_all | solution.py:90
  160.5 9.1 %reshape.304 = f32[1280,64,16]{0,1,2:T(8,128)} reshape(f32[16,80,64,16]{1,0,2,3:T(8,128)} %copy.36) | data formatting | bytes 10485760 | tf_op jit(solution)/shard_map/all_to_all | solution.py:90
  169.6 7.2 %all-to-all-start.1 = ((f32[1280,64,16]{0,1,2:T(8,128)}), f32[1280,64,16]{0,1,2:T(8,128)}, u32[]{:S(2)}, u32[]{:S(2)}) async-start(f32[1280,64,16]{0,1,2:T(8,128)} %reshape.304), calls=%async_computation.1 | async-start | bytes 10485760 | tf_op jit(solution)/shard_map/all_to_all | solution.py:89
  177.0 60.0 %all-to-all-done.1 = f32[1280,64,16]{0,1,2:T(8,128)} async-done(((f32[1280,64,16]{0,1,2:T(8,128)}), f32[1280,64,16]{0,1,2:T(8,128)}, u32[]{:S(2)}, u32[]{:S(2)}) %all-to-all-start.1) | async-done | bytes 5242912 | tf_op jit(solution)/shard_map/all_to_all | solution.py:89
  237.0 5.3 copy.33
  242.4 277.8 %while.14 = (s32[]{:T(128)}, f32[2,8,5248]{2,0,1:T(2,128)}, s32[2]{0:T(128)S(1)}, s32[1280]{0:T(1024)S(1)}, f32[2,1280,512]{1,2,0:T(8,128)}, /*index=5*/s32[8]{0...) while((s32[]{:T(128)}, f32[2,8,5248]{2,0,1:T(2,128)}, ...), condition=%wide.region_3.4_spmd.clone, body=%wide.region_0.3_spmd.clone.sunk | while | flops 10427138048 | bytes 142155696 | solution.py:108
  242.6 0.6 dynamic_slice.34
  244.9 18.0 %fusion.83 = (f32[64,5248]{1,0:T(8,128)S(1)}, f32[64,5248]{1,0:T(8,128)S(1)}) fusion(f32[]{:T(128)S(6)} %div.27, s32[]{:T(128)S(6)} %select_n.194, pred[]{:T(512)S(6)} %lt.178), kind=kLoop, calls=%fused_computation.15.clone.1 | loop fusion | flops 3358720 | bytes 2686985 | tf_op jit(solution)/shard_map/while/body/eval_jaxpr/sin | solution.py:27
  262.9 6.9 %fusion.84 = (f32[20,5248]{1,0:T(8,128)S(1)}, f32[20,5248]{1,0:T(8,128)S(1)}) fusion(f32[]{:T(128)S(6)} %div.27, s32[]{:T(128)S(6)} %select_n.194, s32[20]{0:T(128)S(1)} %iota_multiply_fusion.2, pred[]{:T(512)S(6)} %lt.178), kind=kLoop, calls=%fused_computation.31.clone.1 | loop fusion | flops 1049600 | bytes 839769 | tf_op jit(solution)/shard_map/while/body/eval_jaxpr/cos | solution.py:28
  269.8 18.0 %multiply_add_fusion.2 = (f32[20,64,5248]{2,1,0:T(8,128)}, f32[20,64,5248]{2,1,0:T(8,128)}) fusion(f32[64,5248]{1,0:T(8,128)S(1)} %get-tuple-element.221, f32[20,5248]{1,0:T(8,128)S(1)} %get-tuple-element.222, f32[64,5248]{1,0:T(8,128)S(1)} %get-tuple-element.223, f32[20,5248]{1,0:T(8,128)S(1)} %get-tuple-element.224), kind=kLoop, calls=%fused_computation.2.clone.1 | loop fusion | flops 40304640 | bytes 57266176 | tf_op jit(solution)/shard_map/while/body/eval_jaxpr/add | solution.py:31
  288.4 1.9 constant_dynamic-slice_fusion.2
  290.3 2.9 fusion.81
  293.4 0.4 reshape.315
  293.8 1.4 copy.50
  295.6 33.1 %scatter_fusion = f32[1280,64,2]{1,2,0:T(2,128)S(1)} fusion(f32[1280,64,2]{1,2,0:T(2,128)S(1)} %broadcast.508, s32[1280]{0:T(1024)S(1)} %fusion.80, f32[1280,64,2]{1,2,0:T(2,128)S(1)} %copy.50), kind=kCustom, calls=%fused_computation.clone.clone.1 | custom fusion | bytes 1971200 | tf_op jit(solution)/shard_map/while/body/eval_jaxpr/scatter | solution.py:35
  328.7 3.6 broadcast_multiply_fusion.2
  332.3 1.1 fusion.82
  333.4 20.9 %fusion.85 = f32[64,5248]{1,0:T(8,128)S(1)} fusion(f32[1280,64]{1,0:T(8,128)S(1)} %bitcast.65, f32[1280,5248]{1,0:T(8,128)} %bitcast.62), kind=kOutput, calls=%fused_computation.83.clone.1 | convolution fusion | flops 5158993920 | bytes 28540928 | tf_op jit(solution)/shard_map/while/body/eval_jaxpr/dot_general | solution.py:36
  354.3 0.6 iota_compare_fusion.10
  354.9 21.1 %fusion.86 = f32[64,5248]{1,0:T(8,128)S(1)} fusion(f32[64,5248]{1,0:T(8,128)S(1)} %fusion.85, f32[1280,64]{1,0:T(8,128)S(1)} %bitcast.64, f32[1280,5248]{1,0:T(8,128)} %bitcast.61, pred[5248]{0:T(1024)(128)(4,1)S(1)} %iota_compare_fusion.10), kind=kOutput, calls=%fused_computation.5.clone.1 | convolution fusion | flops 5159665664 | bytes 29889664 | tf_op jit(solution)/shard_map/while/body/eval_jaxpr/dot_general | solution.py:43
  376.0 0.4 reshape.316
  376.4 0.5 fusion.87
  377.1 3.4 dynamic_update_slice.10
  380.9 0.6 dynamic_slice.34
  383.2 17.8 %fusion.83 = (f32[64,5248]{1,0:T(8,128)S(1)}, f32[64,5248]{1,0:T(8,128)S(1)}) fusion(f32[]{:T(128)S(6)} %div.27, s32[]{:T(128)S(6)} %select_n.194, pred[]{:T(512)S(6)} %lt.178), kind=kLoop, calls=%fused_computation.15.clone.1 | loop fusion | flops 3358720 | bytes 2686985 | tf_op jit(solution)/shard_map/while/body/eval_jaxpr/sin | solution.py:27
  401.0 6.9 %fusion.84 = (f32[20,5248]{1,0:T(8,128)S(1)}, f32[20,5248]{1,0:T(8,128)S(1)}) fusion(f32[]{:T(128)S(6)} %div.27, s32[]{:T(128)S(6)} %select_n.194, s32[20]{0:T(128)S(1)} %iota_multiply_fusion.2, pred[]{:T(512)S(6)} %lt.178), kind=kLoop, calls=%fused_computation.31.clone.1 | loop fusion | flops 1049600 | bytes 839769 | tf_op jit(solution)/shard_map/while/body/eval_jaxpr/cos | solution.py:28
  407.9 18.0 %multiply_add_fusion.2 = (f32[20,64,5248]{2,1,0:T(8,128)}, f32[20,64,5248]{2,1,0:T(8,128)}) fusion(f32[64,5248]{1,0:T(8,128)S(1)} %get-tuple-element.221, f32[20,5248]{1,0:T(8,128)S(1)} %get-tuple-element.222, f32[64,5248]{1,0:T(8,128)S(1)} %get-tuple-element.223, f32[20,5248]{1,0:T(8,128)S(1)} %get-tuple-element.224), kind=kLoop, calls=%fused_computation.2.clone.1 | loop fusion | flops 40304640 | bytes 57266176 | tf_op jit(solution)/shard_map/while/body/eval_jaxpr/add | solution.py:31
  426.5 1.9 constant_dynamic-slice_fusion.2
  428.4 2.9 fusion.81
  431.9 1.4 copy.50
  433.7 33.1 %scatter_fusion = f32[1280,64,2]{1,2,0:T(2,128)S(1)} fusion(f32[1280,64,2]{1,2,0:T(2,128)S(1)} %broadcast.508, s32[1280]{0:T(1024)S(1)} %fusion.80, f32[1280,64,2]{1,2,0:T(2,128)S(1)} %copy.50), kind=kCustom, calls=%fused_computation.clone.clone.1 | custom fusion | bytes 1971200 | tf_op jit(solution)/shard_map/while/body/eval_jaxpr/scatter | solution.py:35
  466.8 3.6 broadcast_multiply_fusion.2
  470.4 1.1 fusion.82
  471.5 21.1 %fusion.85 = f32[64,5248]{1,0:T(8,128)S(1)} fusion(f32[1280,64]{1,0:T(8,128)S(1)} %bitcast.65, f32[1280,5248]{1,0:T(8,128)} %bitcast.62), kind=kOutput, calls=%fused_computation.83.clone.1 | convolution fusion | flops 5158993920 | bytes 28540928 | tf_op jit(solution)/shard_map/while/body/eval_jaxpr/dot_general | solution.py:36
  492.6 0.6 iota_compare_fusion.10
  493.2 21.1 %fusion.86 = f32[64,5248]{1,0:T(8,128)S(1)} fusion(f32[64,5248]{1,0:T(8,128)S(1)} %fusion.85, f32[1280,64]{1,0:T(8,128)S(1)} %bitcast.64, f32[1280,5248]{1,0:T(8,128)} %bitcast.61, pred[5248]{0:T(1024)(128)(4,1)S(1)} %iota_compare_fusion.10), kind=kOutput, calls=%fused_computation.5.clone.1 | convolution fusion | flops 5159665664 | bytes 29889664 | tf_op jit(solution)/shard_map/while/body/eval_jaxpr/dot_general | solution.py:43
  514.3 0.4 reshape.316
  514.7 0.5 fusion.87
  515.4 3.4 dynamic_update_slice.10
  520.2 4.2 all-to-all-start.2
  524.5 7.1 %all-to-all-done.2 = f32[8,2,5248]{2,1,0:T(2,128)S(1)} async-done(((f32[8,2,5248]{2,1,0:T(2,128)}), f32[8,2,5248]{2,1,0:T(2,128)S(1)}, u32[]{:S(2)}, u32[]{:S(2)}) %all-to-all-start.2) | async-done | bytes 335904 | tf_op jit(solution)/shard_map/all_to_all | solution.py:110
  531.9 0.8 subtract_select_fusion
  (40 shorter events, 2.8 us)
Async XLA Ops:
  169.6 7.3 %copy-start.4 = (s32[128]{0:T(128)S(1)}, s32[128]{0:T(128)}, u32[]{:S(2)}) copy-start(s32[128]{0:T(128)} %param.12) | copy-start | bytes 1540
  169.6 7.4 %copy-start.2 = (s32[8]{0:T(128)S(1)}, s32[8]{0:T(128)}, u32[]{:S(2)}) copy-start(s32[8]{0:T(128)} %param.13) | copy-start | bytes 100
  169.6 7.4 %copy-start.3 = (f32[8]{0:T(128)S(1)}, f32[8]{0:T(128)}, u32[]{:S(2)}) copy-start(f32[8]{0:T(128)} %param.14) | copy-start | bytes 100
  169.6 67.4 %all-to-all-start.1 = ((f32[1280,64,16]{0,1,2:T(8,128)}), f32[1280,64,16]{0,1,2:T(8,128)}, u32[]{:S(2)}, u32[]{:S(2)}) async-start(f32[1280,64,16]{0,1,2:T(8,128)} %reshape.304), calls=%async_computation.1 | async-start | bytes 10485760 | tf_op jit(solution)/shard_map/all_to_all | solution.py:89
  176.9 65.5 %copy-start.5 = (s32[256]{0:T(256)}, s32[256]{0:T(256)S(1)}, u32[]{:S(2)}) copy-start(s32[256]{0:T(256)S(1)} %constant_dynamic-update-slice_fusion) | copy-start | bytes 3076
  237.0 5.3 copy-start.1
  242.3 282.0 %copy-start.6 = (s32[256]{0:T(256)S(1)}, s32[256]{0:T(256)}, u32[]{:S(2)}) copy-start(s32[256]{0:T(256)} %copy-done.5) | copy-start | bytes 3076
  242.3 289.5 %copy-start = (f32[1,16,5248]{2,1,0:T(8,128)S(1)}, f32[1,16,5248]{2,1,0:T(8,128)}, u32[]{:S(2)}) copy-start(f32[1,16,5248]{2,1,0:T(8,128)} %param.15) | copy-start | bytes 1007620
  520.2 11.4 %all-to-all-start.2 = ((f32[8,2,5248]{2,1,0:T(2,128)}), f32[8,2,5248]{2,1,0:T(2,128)S(1)}, u32[]{:S(2)}, u32[]{:S(2)}) async-start(f32[8,2,5248]{2,1,0:T(2,128)} %bitcast.7), calls=%async_computation.2 | async-start | bytes 671744 | tf_op jit(solution)/shard_map/all_to_all | solution.py:110
where the time goes:
time: 538 us; the launch traced here: 533 us
  matrix products  123 us (23%)
  local copies, waits for them, and re-layouts  119 us (22%)
  blocking collectives  103 us (19%)
  other arithmetic  101 us (19%)
  waiting for transfers between devices  67.2 us (12%)
  starting transfers between devices  11.5 us (2%)
  loops' own time  6.9 us (1%)
    all_to_all x1, blocking collectives, local(): lax.all_to_all(fourier, 'wave', split_axis=2, concat_axis=0, tiled=True)  103 us
    scatter x2, local copies, waits for them, and re-layouts, synthesize(): jnp.zeros_like(coeffs).at[wave_map].set(coeffs) * factor[:, None, None]  66.2 us
    all_to_all x1, waiting for transfers between devices, local(): lax.all_to_all(lax.all_to_all(fourier, 'wave', split_axis=2, concat_axis=...  60 us
    dot_general x2, matrix products, synthesize(): lax.dot_general(ordered[:, :, 1], sine_part, (((0,), (0,)), ((), ())), pr...  42.2 us
    dot_general x2, matrix products, synthesize(): lax.dot_general(ordered[:, :, 0], cosine, (((0,), (0,)), ((), ())), preci...  41.9 us
    add x2, other arithmetic, synthesize(): coarse_sin * fine_cos + coarse_cos * fine_sin  35.9 us
    sin x2, other arithmetic, synthesize(): fine_sin = jnp.sin(fine_angle)[None, :, :]  35.8 us
    all_to_all x2, local copies, waits for them, and re-layouts, local(): lax.all_to_all(fourier, 'wave', split_axis=2, concat_axis=0, tiled=True)  18.9 us
  transfers between devices with their start and end apart: 2, of which 2 were waited for; matrix products, arithmetic and copies ran while one was open for 0% of the time, Pallas kernels for 0%

commit v1 on v0

v1 whole, which is shorter than its diff:
```python
import functools
import math

import jax
import jax.numpy as jnp
from jax import lax
from jax.experimental import pallas as pl
from jax.experimental.pallas import tpu as pltpu
from jax.sharding import PartitionSpec as P

MESH = pl.DeviceIdType.MESH

M = 1280
NT = 1280
LEV_DEV = 4
COLS = 16
HALF = 128
ROWPAD = 5248
LANES = 128

WAVES = 16
LEVS = 8
DEVICES = WAVES * LEVS
SLOTS = M // WAVES
STEP_SLOTS = 8
STEPS = SLOTS // STEP_SLOTS
GROUPS = SLOTS // 4
PACK = 24
PER_SLOT = 2 * COLS

KBLOCK = 128
KBLOCKS = 11
KSPAN = KBLOCK * KBLOCKS
TILES = ROWPAD // LANES
ROWTILES = 48

NT_DIMS = (((1,), (1,)), ((), ()))


def flat_id():
    return lax.axis_index("wave") * LEVS + lax.axis_index("lev")


def pair_of(wave, lev):
    return (wave % 8) * 16 + (wave // 8) * 8 + lev


def transform_kernel(
    waves_ref, brackets_ref, weight_ref, spec_ref, leg_ref, recv_ref,
    mixed, first, other, send, near_send, near_recv, far_send, far_recv, own_sem,
):
    step = pl.program_id(0)
    wave, lev = lax.axis_index("wave"), lax.axis_index("lev")
    me = wave * LEVS + lev
    below = lax.rem(lev + LEVS - 1, LEVS)
    barrier = pltpu.get_barrier_semaphore()

    @pl.when(step == 0)
    def _():
        def greet(d, carry):
            target = lax.rem(me + d, DEVICES)
            pl.semaphore_signal(
                barrier, inc=1, device_id=(target // LEVS, lax.rem(target, LEVS)), device_id_type=MESH
            )
            return carry

        lax.fori_loop(1, DEVICES, greet, 0)
        for g in range(GROUPS, PACK):
            send[pl.ds(g, HALF, stride=PACK), :] = jnp.zeros((HALF, LANES), jnp.float32)

    lower = brackets_ref[lev] - lev * LEV_DEV
    weight = weight_ref[lev]
    level_weight = []
    for level in range(LEV_DEV):
        share = jnp.where(lower == level, weight, 0.0) + jnp.where(lower + 1 == level, 1.0 - weight, 0.0)
        level_weight.append(share)
    gain = jnp.where(lower == LEV_DEV - 1, 1.0 - weight, 0.0)

    degree = lax.broadcasted_iota(jnp.int32, (1, NT), 1)
    for i in range(STEP_SLOTS):
        order = waves_ref[wave * SLOTS + step * STEP_SLOTS + i]
        kept = jnp.where(degree >= order, 1.0, 0.0)
        signed = kept * (1 - 2 * ((degree + order) & 1)).astype(jnp.float32)
        coeffs = spec_ref[i]
        both = jnp.concatenate(
            [coeffs * kept.astype(jnp.bfloat16), coeffs * signed.astype(jnp.bfloat16)], axis=0
        )
        sums = lax.dot_general(both, leg_ref[i], NT_DIMS, preferred_element_type=jnp.float32)
        base = (step * STEP_SLOTS + i) * PER_SLOT
        for hemi in range(2):
            own = [sums[(hemi * LEV_DEV + v) * COLS : (hemi * LEV_DEV + v + 1) * COLS] for v in range(LEV_DEV)]
            total = own[0] * level_weight[0]
            for v in range(1, LEV_DEV):
                total = total + own[v] * level_weight[v]
            at = pl.ds(pl.multiple_of(base + hemi * COLS, COLS), COLS)
            mixed[at, :] = total
            first[at, :] = own[0]

    def near_copy(t):
        rows = pl.ds(pl.multiple_of(t * (STEP_SLOTS * PER_SLOT), STEP_SLOTS * PER_SLOT), STEP_SLOTS * PER_SLOT)
        return pltpu.make_async_remote_copy(
            src_ref=first.at[rows],
            dst_ref=other.at[rows],
            send_sem=near_send.at[t],
            recv_sem=near_recv.at[t],
            device_id=(wave, below),
            device_id_type=MESH,
        )

    @pl.when(step == 0)
    def _():
        pl.semaphore_wait(barrier, DEVICES - 1)

    near_copy(step).start()

    def assemble(g, carry):
        pieces = []
        for c in range(8):
            b = lax.rem(c - lev + 8, 8)
            base = (4 * g + b // 2) * PER_SLOT + lax.rem(b, 2)
            for hemi in range(2):
                at = pl.ds(base + hemi * COLS, 8, stride=2)
                pieces.append(mixed[at, :] + gain * other[at, :])
        block = jnp.concatenate(pieces, axis=0)
        send[pl.ds(g, HALF, stride=PACK), :] = block.T
        return carry

    @pl.when(step == STEPS - 1)
    def _():
        for t in range(STEPS):
            near_copy(t).wait_recv()
            lax.fori_loop(2 * t, 2 * t + 2, assemble, 0)

        def far_copy(d):
            target = lax.rem(me + d, DEVICES)
            to_wave, to_lev = target // LEVS, lax.rem(target, LEVS)
            at = pl.multiple_of(pair_of(to_wave, to_lev) * PACK, 8)
            return pltpu.make_async_remote_copy(
                src_ref=send.at[pl.ds(at, PACK)],
                dst_ref=recv_ref.at[me],
                send_sem=far_send,
                recv_sem=far_recv,
                device_id=(to_wave, to_lev),
                device_id_type=MESH,
            )

        def push(d, carry):
            far_copy(d).start()
            return carry

        lax.fori_loop(1, DEVICES, push, 0)
        mine = pltpu.make_async_copy(
            send.at[pl.ds(pl.multiple_of(pair_of(wave, lev) * PACK, 8), PACK)], recv_ref.at[me], own_sem
        )
        mine.start()
        mine.wait()
        for t in range(STEPS):
            near_copy(t).wait_send()
        all_out = send.at[pl.ds(0, (DEVICES - 1) * PACK)]
        pltpu.make_async_copy(all_out, all_out, far_send).wait()
        all_in = recv_ref.at[pl.ds(0, DEVICES - 1)]
        pltpu.make_async_copy(all_in, all_in, far_recv).wait()


def transform(wave_map, brackets, lev_weight, spectral, legendre):
    smem = pl.BlockSpec(memory_space=pltpu.SMEM)
    rows = SLOTS * PER_SLOT
    return pl.pallas_call(
        transform_kernel,
        grid=(STEPS,),
        out_shape=jax.ShapeDtypeStruct((DEVICES, PACK, LANES), jnp.float32),
        in_specs=[
            smem,
            smem,
            smem,
            pl.BlockSpec((STEP_SLOTS, LEV_DEV * COLS, NT), lambda t: (t, 0, 0)),
            pl.BlockSpec((STEP_SLOTS, HALF, NT), lambda t: (t, 0, 0)),
        ],
        out_specs=pl.BlockSpec(memory_space=pl.ANY),
        scratch_shapes=[
            pltpu.VMEM((rows, HALF), jnp.float32),
            pltpu.VMEM((rows, HALF), jnp.float32),
            pltpu.VMEM((rows, HALF), jnp.float32),
            pltpu.VMEM((HALF * PACK, LANES), jnp.float32),
            pltpu.SemaphoreType.DMA((STEPS,)),
            pltpu.SemaphoreType.DMA((STEPS,)),
            pltpu.SemaphoreType.DMA,
            pltpu.SemaphoreType.DMA,
            pltpu.SemaphoreType.DMA,
        ],
        compiler_params=pltpu.CompilerParams(
            collective_id=0, has_side_effects=True, vmem_limit_bytes=48 * 1024 * 1024
        ),
        name="transform",
    )(wave_map, brackets, lev_weight, spectral, legendre)


def turn(product, points):
    inverse = 1.0 / points
    rest = product - jnp.floor(product * inverse + 0.5) * points
    x = rest * (math.pi * inverse)
    y = x * x
    sine = x * (
        1.0
        + y * (-1.0 / 6 + y * (1.0 / 120 + y * (-1.0 / 5040 + y * (1.0 / 362880 - y * (1.0 / 39916800)))))
    )
    cosine = 1.0 + y * (
        -0.5
        + y * (1.0 / 24 + y * (-1.0 / 720 + y * (1.0 / 40320 + y * (-1.0 / 3628800 + y * (1.0 / 479001600)))))
    )
    return 1.0 - 2.0 * (sine * sine), 2.0 * (sine * cosine)


def halves(x):
    high = x.astype(jnp.bfloat16)
    return high, (x - high.astype(jnp.float32)).astype(jnp.bfloat16)


def synthesis_kernel(
    points_ref, recv_ref, orders_ref, sign_ref, out_ref,
    coef, re_hi, re_lo, im_hi, im_lo, fine_c, fine_s, coarse_c, coarse_s, cand,
):
    count = points_ref[0]
    points = count.astype(jnp.float32)
    lane_block = lax.broadcasted_iota(jnp.int32, (8, LANES), 1) // COLS
    bits = [((lane_block >> t) & 1) == 1 for t in range(3)]
    for w in range(WAVES):
        for i0 in range(0, GROUPS, 8):
            keep = min(8, GROUPS - i0)
            held = [recv_ref[w * LEVS + p, i0 : i0 + 8, :] for p in range(LEVS)]
            for t in range(3):
                held = [jnp.where(bits[t], held[(x + (1 << t)) % 8], held[x]) for x in range(8)]
            for b in range(8):
                moved = held[-b % 8]
                if b:
                    moved = pltpu.roll(moved, LANES - COLS * b, 1)
                coef[b, w * GROUPS + i0 : w * GROUPS + i0 + keep, :] = moved[:keep]
    span = WAVES * GROUPS
    for u in range(4):
        at = slice(u * span, (u + 1) * span)
        sign = sign_ref[at, :]
        for part, (high_ref, low_ref) in enumerate(((re_hi, re_lo), (im_hi, im_lo))):
            plain = coef[2 * u + part]
            for side, value in enumerate((plain, plain * sign)):
                high, low = halves(value)
                high_ref[at, side * LANES : (side + 1) * LANES] = high
                low_ref[at, side * LANES : (side + 1) * LANES] = low

    orders = orders_ref[...]
    fine_k = lax.broadcasted_iota(jnp.int32, (KBLOCK, 1), 0).astype(jnp.float32)
    fine_c[...], fine_s[...] = turn(fine_k * orders, points)
    coarse_k = lax.broadcasted_iota(jnp.int32, (16, 1), 0).astype(jnp.float32) * KBLOCK
    factor = jnp.where(orders == 0.0, 1.0, 2.0)
    factor = jnp.where(orders <= ((count - 1) // 2).astype(jnp.float32), factor, 0.0)
    whole_c, whole_s = turn(coarse_k * orders, points)
    coarse_c[...] = whole_c * factor
    coarse_s[...] = whole_s * factor

    row = lax.broadcasted_iota(jnp.int32, (64, 4 * LANES), 0)
    col = lax.broadcasted_iota(jnp.int32, (64, 4 * LANES), 1)
    belongs = ((row >> 4) == (col >> 7)) & ((row & 7) == ((col >> 4) & 7)) & (((row >> 3) & 1) == ((col >> 3) & 1))
    gather = jnp.where(belongs, 0.125, 0.0).astype(jnp.bfloat16)
    flip_row = lax.broadcasted_iota(jnp.int32, (LANES, LANES), 0)
    flip_col = lax.broadcasted_iota(jnp.int32, (LANES, LANES), 1)
    flip = jnp.where(flip_row + flip_col == LANES - 1, 1.0, 0.0).astype(jnp.bfloat16)

    quarter = count // 4
    offsets = (0, 2 * quarter - (KSPAN - 1), 2 * quarter, 4 * quarter - (KSPAN - 1))
    shifts = [lax.rem(off + KSPAN, LANES) for off in offsets]
    heads = [(off + KSPAN) // LANES - KBLOCKS for off in offsets]

    def block(a, carry):
        cc, cs = coarse_c[pl.ds(a, 1), :], coarse_s[pl.ds(a, 1), :]
        fc, fs = fine_c[...], fine_s[...]
        dot = functools.partial(jnp.dot, preferred_element_type=jnp.float32)
        cos_hi, cos_lo = halves(fc * cc - fs * cs)
        real = dot(cos_hi, re_hi[...]) + dot(cos_lo, re_hi[...]) + dot(cos_hi, re_lo[...])
        sin_hi, sin_lo = halves(fs * cc + fc * cs)
        imag = dot(sin_hi, im_hi[...]) + dot(sin_lo, im_hi[...]) + dot(sin_hi, im_lo[...])
        p, q = real[:, :LANES], real[:, LANES:]
        r, s = imag[:, :LANES], imag[:, LANES:]
        values = jnp.concatenate([p - r, q + s, q - s, p + r], axis=1)
        sq_hi, sq_lo = halves(values * values)
        energy = lax.dot_general(gather, sq_hi, NT_DIMS, preferred_element_type=jnp.float32)
        energy = energy + lax.dot_general(gather, sq_lo, NT_DIMS, preferred_element_type=jnp.float32)
        e_hi, e_lo = halves(energy)
        back = dot(e_hi, flip) + dot(e_lo, flip)
        for x in range(4):
            tile = (back if x % 2 else energy)[16 * x : 16 * x + 16]
            place = (KBLOCKS - 1 - a) if x % 2 else a
            cand[x, place] = pltpu.roll(tile, shifts[x], 1) if x else tile
        return carry

    lax.fori_loop(0, KBLOCKS, block, 0)

    lane = lax.broadcasted_iota(jnp.int32, (16, LANES), 1)

    def finish(t, carry):
        place = t * LANES + lane
        picked = []
        for x in range(4):
            here = jnp.clip(t - heads[x], 0, KBLOCKS - 1)
            before = jnp.clip(t - heads[x] - 1, 0, KBLOCKS - 1)
            picked.append(jnp.where(lane >= shifts[x], cand[x, here], cand[x, before]))
        value = jnp.where(place < count, picked[3], 0.0)
        value = jnp.where(place <= 3 * quarter, picked[2], value)
        value = jnp.where(place <= 2 * quarter, picked[1], value)
        value = jnp.where(place <= quarter, picked[0], value)
        out_ref[pl.ds(t, 16, stride=ROWTILES), :] = value
        return carry

    lax.fori_loop(0, TILES, finish, 0)
    for t in range(TILES, ROWTILES):
        out_ref[pl.ds(t, 16, stride=ROWTILES), :] = jnp.zeros((16, LANES), jnp.float32)


def synthesis(points, recv, orders, sign):
    vmem = pl.BlockSpec(memory_space=pltpu.VMEM)
    return pl.pallas_call(
        synthesis_kernel,
        out_shape=jax.ShapeDtypeStruct((16 * ROWTILES, LANES), jnp.float32),
        in_specs=[pl.BlockSpec(memory_space=pltpu.SMEM), vmem, vmem, vmem],
        out_specs=vmem,
        scratch_shapes=[
            pltpu.VMEM((8, WAVES * GROUPS, LANES), jnp.float32),
            pltpu.VMEM((M, 2 * LANES), jnp.bfloat16),
            pltpu.VMEM((M, 2 * LANES), jnp.bfloat16),
            pltpu.VMEM((M, 2 * LANES), jnp.bfloat16),
            pltpu.VMEM((M, 2 * LANES), jnp.bfloat16),
            pltpu.VMEM((KBLOCK, M), jnp.float32),
            pltpu.VMEM((KBLOCK, M), jnp.float32),
            pltpu.VMEM((16, M), jnp.float32),
            pltpu.VMEM((16, M), jnp.float32),
            pltpu.VMEM((4, KBLOCKS, 16, LANES), jnp.float32),
        ],
        compiler_params=pltpu.CompilerParams(vmem_limit_bytes=48 * 1024 * 1024),
        name="synthesis",
    )(points, recv, orders, sign)


def back_kernel(points_ref, energy_ref, clim_ref, out_ref, got, send_sem, recv_sem, own_sem):
    wave, lev = lax.axis_index("wave"), lax.axis_index("lev")
    half, base = wave // 8, lax.rem(wave, 8)
    member = half * LEVS + lev
    barrier = pltpu.get_barrier_semaphore()

    def device(k):
        return base + 8 * (k // LEVS), lax.rem(k, LEVS)

    def greet(d, carry):
        pl.semaphore_signal(barrier, inc=1, device_id=device(lax.rem(member + d, 16)), device_id_type=MESH)
        return carry

    lax.fori_loop(1, 16, greet, 0)
    pl.semaphore_wait(barrier, 15)

    def rows(k):
        return pl.ds(pl.multiple_of(k * ROWTILES, 8), ROWTILES)

    def push(d, carry):
        k = lax.rem(member + d, 16)
        pltpu.make_async_remote_copy(
            src_ref=energy_ref.at[rows(k)],
            dst_ref=got.at[rows(member)],
            send_sem=send_sem,
            recv_sem=recv_sem,
            device_id=device(k),
            device_id_type=MESH,
        ).start()
        return carry

    lax.fori_loop(1, 16, push, 0)
    mine = pltpu.make_async_copy(energy_ref.at[rows(member)], got.at[rows(member)], own_sem)
    mine.start()
    mine.wait()
    part = pl.ds(0, 15 * ROWTILES)
    pltpu.make_async_copy(energy_ref.at[part], energy_ref.at[part], send_sem).wait()
    pltpu.make_async_copy(got.at[part], got.at[part], recv_sem).wait()

    row = lax.broadcasted_iota(jnp.int32, (16, LANES), 0)
    lane = lax.broadcasted_iota(jnp.int32, (16, LANES), 1)
    count = jnp.zeros((16, LANES), jnp.int32)
    for r in range(16):
        count = jnp.where(row == r, points_ref[base * 16 + r], count)
    for t in range(TILES):
        at = slice(t * LANES, (t + 1) * LANES)
        value = got[pl.ds(t, 16, stride=ROWTILES), :] - clim_ref[0, :, at]
        out_ref[0, :, at] = jnp.where(lane + t * LANES < count, value, 0.0)


def back(row_points, energy, climatology):
    vmem = pl.BlockSpec(memory_space=pltpu.VMEM)
    return pl.pallas_call(
        back_kernel,
        out_shape=jax.ShapeDtypeStruct((1, 16, ROWPAD), jnp.float32),
        in_specs=[pl.BlockSpec(memory_space=pltpu.SMEM), vmem, vmem],
        out_specs=vmem,
        scratch_shapes=[
            pltpu.VMEM((16 * ROWTILES, LANES), jnp.float32),
            pltpu.SemaphoreType.DMA,
            pltpu.SemaphoreType.DMA,
            pltpu.SemaphoreType.DMA,
        ],
        compiler_params=pltpu.CompilerParams(
            collective_id=1, has_side_effects=True, vmem_limit_bytes=32 * 1024 * 1024
        ),
        name="back",
    )(row_points, energy, climatology)


def local(spectral, legendre, wave_map, row_points, brackets, lev_weight, climatology):
    wave, lev = lax.axis_index("wave"), lax.axis_index("lev")
    recv = transform(wave_map, brackets, lev_weight, spectral, legendre)
    ordered = jnp.transpose(wave_map.reshape(WAVES, GROUPS, 4), (2, 0, 1))
    orders = ordered.reshape(1, M).astype(jnp.float32)
    sign = (1 - 2 * (ordered & 1)).astype(jnp.float32).reshape(M, 1)
    points = lax.dynamic_slice_in_dim(row_points, pair_of(wave, lev), 1, 0)
    energy = synthesis(points, recv, orders, sign)
    return back(row_points, energy, climatology)


def solution(mesh):
    placed = (
        P("wave", "lev", None),
        P("wave", None, None),
        P(),
        P(),
        P(),
        P(),
        P("lev", "wave", None),
    )
    return jax.shard_map(
        local, mesh=mesh, in_specs=placed, out_specs=P("lev", "wave", None), check_vma=False
    )
```

time: 538 us -> 86.8 us (0.16)
  matrix products: 123 us -> 0 us
  local copies, waits for them, and re-layouts: 119 us -> 4.99 us
  blocking collectives: 103 us -> 0 us
  other arithmetic: 101 us -> 0.78 us
  Pallas kernels: 0 us -> 80.6 us
  waiting for transfers between devices: 67.2 us -> 0 us
  starting transfers between devices: 11.5 us -> 0 us
  loops' own time: 6.9 us -> 0 us
    dot_general x8 -> x0, matrix products: 123 us -> none  [the longest x2 42.2 us: synthesize(): lax.dot_general(ordered[:, :, 1], sine_part, (((0,), (0,)), ((), ())), pr...]
    all_to_all x1 -> x0, blocking collectives: 103 us -> none  [local(): lax.all_to_all(fourier, 'wave', split_axis=2, concat_axis=0, tiled=True)]
    pallas_call x0 -> x3, Pallas kernels: none -> 80.6 us  [the longest x1 52.7 us: transform(): pl.pallas_call(transform_kernel, grid=(STEPS,), out_shape=jax.ShapeDtypeS...]
    all_to_all x2 -> x0, waiting for transfers between devices: 67.2 us -> none  [the longest x1 60 us: local(): lax.all_to_all(lax.all_to_all(fourier, 'wave', split_axis=2, concat_axis=...]
    scatter x2 -> x0, local copies, waits for them, and re-layouts: 66.2 us -> none  [synthesize(): jnp.zeros_like(coeffs).at[wave_map].set(coeffs) * factor[:, None, None]]
    add x3 -> x0, other arithmetic: 35.9 us -> none  [the longest x2 35.9 us: synthesize(): coarse_sin * fine_cos + coarse_cos * fine_sin]
    sin x2 -> x0, other arithmetic: 35.8 us -> none  [synthesize(): fine_sin = jnp.sin(fine_angle)[None, :, :]]
    all_to_all x4 -> x0, local copies, waits for them, and re-layouts: 24.4 us -> none  [the longest x2 18.9 us: local(): lax.all_to_all(fourier, 'wave', split_axis=2, concat_axis=0, tiled=True)]
  transfers between devices with their start and end apart: 2 -> 0, of which waited for: 2 -> 0; matrix products, arithmetic and copies ran while one was open for 0% -> 0% of each run, Pallas kernels for 0% -> 0%
where the time goes in v1:
time: 86.8 us; the launch traced here: 86.5 us
  Pallas kernels  80.6 us (93%)
  local copies, waits for them, and re-layouts  4.99 us (6%)
    pallas_call x1, Pallas kernels, transform(): pl.pallas_call(transform_kernel, grid=(STEPS,), out_shape=jax.ShapeDtypeS...  52.7 us
    pallas_call x1, Pallas kernels, synthesis(): pl.pallas_call(synthesis_kernel, out_shape=jax.ShapeDtypeStruct((16 * ROW...  16.9 us
    pallas_call x1, Pallas kernels, back(): pl.pallas_call(back_kernel, out_shape=jax.ShapeDtypeStruct((1, 16, ROWPAD...  11.1 us
    unnamed x11, local copies, waits for them, and re-layouts  2.74 us

profile of v1, /device:TPU:1, one launch (start us, length us, event | category | flops | bytes accessed | tf_op | source)
XLA Modules:
  0.0 86.5 jit_solution(6978289774017441360)
XLA Ops:
  0.0 1.2 %dynamic_slice.3.points_ref = s32[1]{0:T(128)} dynamic-slice(s32[128]{0:T(128)} %points_ref.1, s32[]{:T(128)S(6)} %select_n.16), dynamic_slice_sizes={1} | dynamic-slice | bytes 12 | tf_op jit(solution)/shard_map/dynamic_slice | solution.py:417
  1.2 0.8 subtract_convert_fusion
  2.0 0.1 reshape.26
  2.2 0.2 copy.9
  2.4 0.1 convert_element_type.13
  2.5 0.2 copy.8
  2.7 0.1 convert_element_type.15.orders_ref
  2.8 0.2 reshape.27.sign_ref
  3.1 0.0 copy-start.1
  3.1 0.7 copy-done.1
  3.8 0.0 copy-start.2
  3.8 0.7 copy-done.2
  4.4 0.0 copy-start.3
  4.4 0.7 copy-done.3
  5.1 0.0 copy-start
  5.1 0.0 copy-start.4
  5.1 52.7 %transform.1.recv_ref = f32[128,24,128]{2,1,0:T(8,128)S(1)} custom-call(s32[1280]{0:T(1024)S(1)} %copy-done.1, s32[8]{0:T(128)S(1)} %copy-done.2, f32[8]{0:T(128)S(1)} %copy-done.3, bf16[80,64,1280]{2,1,0:T(8,128)(2,1)} %spec_ref.1, bf16[80,128,1280]{2,1,0:T(8,128)(2,1)} %leg_ref.1), custom_call_target="tpu_custom_call" | custom-call | tf_op jit(solution)/shard_map/transform/pallas_call | solution.py:168
  57.7 16.9 %synthesis.1.energy_ref = f32[768,128]{1,0:T(8,128)S(1)} custom-call(s32[1]{0:T(128)} %dynamic_slice.3.points_ref, f32[128,24,128]{2,1,0:T(8,128)S(1)} %transform.1.recv_ref, f32[1,1280]{1,0:T(1,128)S(1)} %convert_element_type.15.orders_ref, f32[1280,1]{1,0:T(8,128)S(1)} %reshape.27.sign_ref), custom_call_target="tpu_custom_call" | custom-call | tf_op jit(solution)/shard_map/synthesis/pallas_call | solution.py:319
  74.6 0.0 copy-done
  74.6 0.0 copy-done.4
  74.6 11.1 %back.1 = f32[1,16,5248]{2,1,0:T(8,128)S(1)} custom-call(s32[128]{0:T(128)S(1)} %copy-done.4, f32[768,128]{1,0:T(8,128)S(1)} %synthesis.1.energy_ref, f32[1,16,5248]{2,1,0:T(8,128)S(1)} %copy-done), custom_call_target="tpu_custom_call" | custom-call | tf_op jit(solution)/shard_map/back/pallas_call | solution.py:393
  85.7 0.7 copy.12
Async XLA Ops:
  3.1 0.7 copy-start.1
  3.8 0.7 copy-start.2
  4.4 0.7 copy-start.3
  5.1 69.5 %copy-start = (f32[1,16,5248]{2,1,0:T(8,128)S(1)}, f32[1,16,5248]{2,1,0:T(8,128)}, u32[]{:S(2)}) copy-start(f32[1,16,5248]{2,1,0:T(8,128)} %clim_ref.1) | copy-start | bytes 1007620
  5.1 69.6 %copy-start.4 = (s32[128]{0:T(128)S(1)}, s32[128]{0:T(128)}, u32[]{:S(2)}) copy-start(s32[128]{0:T(128)} %points_ref.1) | copy-start | bytes 1540

commit v2 on v0

v2 whole, which is shorter than its diff:
```python
import functools
import math

import jax
import jax.numpy as jnp
from jax import lax
from jax.experimental import pallas as pl
from jax.experimental.pallas import tpu as pltpu
from jax.sharding import PartitionSpec as P

MESH = pl.DeviceIdType.MESH

M = 1280
NT = 1280
LEV_DEV = 4
COLS = 16
HALF = 128
ROWPAD = 5248
LANES = 128

WAVES = 16
LEVS = 8
DEVICES = WAVES * LEVS
SLOTS = M // WAVES
STEP_SLOTS = 16
STEPS = SLOTS // STEP_SLOTS
STEP_ROWS = STEP_SLOTS * 2 * COLS
PER_SLOT = 2 * COLS
FIRST_ROWS, LAST_ROWS = 16, 8
PACK = FIRST_ROWS + LAST_ROWS
GROUPS = SLOTS // 4
FIRST = WAVES * 64
LAST = WAVES * 16
STRIDE = 37

KBLOCK = 128
KBLOCKS = 11
KSPAN = KBLOCK * KBLOCKS
KWIDE = 352
TILES = ROWPAD // LANES
ROWTILES = 48

NT_DIMS = (((1,), (1,)), ((), ()))


def pair_of(wave, lev):
    return (wave % 8) * 16 + (wave // 8) * 8 + lev


def turn(product, points):
    inverse = 1.0 / points
    rest = product - jnp.floor(product * inverse + 0.5) * points
    x = rest * (math.pi * inverse)
    y = x * x
    sine = x * (
        1.0
        + y * (-1.0 / 6 + y * (1.0 / 120 + y * (-1.0 / 5040 + y * (1.0 / 362880 - y * (1.0 / 39916800)))))
    )
    cosine = 1.0 + y * (
        -0.5
        + y * (1.0 / 24 + y * (-1.0 / 720 + y * (1.0 / 40320 + y * (-1.0 / 3628800 + y * (1.0 / 479001600)))))
    )
    return 1.0 - 2.0 * (sine * sine), 2.0 * (sine * cosine)


def halves(x):
    high = x.astype(jnp.bfloat16)
    return high, (x - high.astype(jnp.float32)).astype(jnp.bfloat16)


def dot(a, b):
    return jnp.dot(a, b, preferred_element_type=jnp.float32)


def kernel(
    waves_ref, brackets_ref, weight_ref, points_ref, orders_ref, spec_ref, leg_ref, out_ref,
    mixed, first, other, send, recv, coef, sign, re_hi, re_lo, im_hi, im_lo,
    fine_c, fine_s, coarse_c, coarse_s, cos_hi, cos_lo, sin_hi, sin_lo, acc, sq_hi, sq_lo, cand, energy_out, got,
    near_send, near_recv, far_send, far_recv, own_sem, back_send, back_recv, ready,
):
    step = pl.program_id(0)
    wave, lev = lax.axis_index("wave"), lax.axis_index("lev")
    me = wave * LEVS + lev
    below = lax.rem(lev + LEVS - 1, LEVS)
    barrier = pltpu.get_barrier_semaphore()

    @pl.when(step == 0)
    def _():
        for d in range(1, LEVS):
            pl.semaphore_signal(
                barrier, inc=1, device_id=(wave, lax.rem(lev + d, LEVS)), device_id_type=MESH
            )
        for d in range(1, WAVES):
            pl.semaphore_signal(
                barrier, inc=1, device_id=(lax.rem(wave + d, WAVES), lev), device_id_type=MESH
            )

    lower = brackets_ref[lev] - lev * LEV_DEV
    weight = weight_ref[lev]
    inside = lower < LEV_DEV - 1
    gain = jnp.where(inside, 0.0, 1.0 - weight)
    level_weight = [
        jnp.where(lower == v, weight, 0.0) + jnp.where(lower + 1 == v, 1.0 - weight, 0.0) for v in range(LEV_DEV)
    ]

    degree = lax.broadcasted_iota(jnp.int32, (1, NT), 1)
    for i in range(STEP_SLOTS):
        order = waves_ref[wave * SLOTS + step * STEP_SLOTS + i]
        kept = jnp.where(degree >= order, 1.0, 0.0)
        signed = kept * (1 - 2 * ((degree + order) & 1)).astype(jnp.float32)
        kept, signed = kept.astype(jnp.bfloat16), signed.astype(jnp.bfloat16)
        coeffs = spec_ref[i]
        both = jnp.concatenate([coeffs * kept, coeffs * signed], axis=0)
        sums = lax.dot_general(both, leg_ref[i], NT_DIMS, preferred_element_type=jnp.float32)
        base = step * STEP_ROWS + i * PER_SLOT
        for hemi in range(2):
            own = [sums[(LEV_DEV * hemi + v) * COLS : (LEV_DEV * hemi + v + 1) * COLS] for v in range(LEV_DEV)]
            at = pl.ds(pl.multiple_of(base + hemi * COLS, COLS), COLS)
            total = own[0] * level_weight[0]
            for v in range(1, LEV_DEV):
                total = total + own[v] * level_weight[v]
            mixed[at, :] = total
            first[at, :] = own[0]

    def near_copy(t):
        rows = pl.ds(pl.multiple_of(t * STEP_ROWS, STEP_ROWS), STEP_ROWS)
        return pltpu.make_async_remote_copy(
            src_ref=first.at[rows],
            dst_ref=other.at[rows],
            send_sem=near_send.at[t],
            recv_sem=near_recv.at[t],
            device_id=(wave, below),
            device_id_type=MESH,
        )

    @pl.when(step == 0)
    def _():
        pl.semaphore_wait(barrier, LEVS + WAVES - 2)
        for d in range(1, LEVS):
            pl.semaphore_signal(
                ready, inc=1, device_id=(wave, lax.rem(lev + d, LEVS)), device_id_type=MESH
            )

    near_copy(step).start()

    def assemble(g, slot_of):
        pieces = []
        for c in range(8):
            b = lax.rem(c - lev + 8, 8)
            base = slot_of(b // 2) * PER_SLOT + lax.rem(b, 2)
            for hemi in range(2):
                at = pl.ds(base + hemi * COLS, 8, stride=2)
                pieces.append(mixed[at, :] + gain * other[at, :])
        block = jnp.concatenate(pieces, axis=0)
        send[pl.ds(g, HALF, stride=PACK), :] = block.T

    def assemble_pair(tau):
        near_copy(2 * tau).wait_recv()
        near_copy(2 * tau + 1).wait_recv()

        def one(r, carry):
            assemble(8 * tau + r, lambda u: 32 * tau + 8 * u + r)
            return carry

        lax.fori_loop(0, 8, one, 0)

    def far_copy(d, start, count, part):
        target = lax.rem(me + STRIDE * d, DEVICES)
        to_wave, to_lev = target // LEVS, lax.rem(target, LEVS)
        at = pl.multiple_of(pair_of(to_wave, to_lev) * PACK + start, 8)
        return pltpu.make_async_remote_copy(
            src_ref=send.at[pl.ds(at, count)],
            dst_ref=recv.at[me, pl.ds(start, count)],
            send_sem=far_send.at[part],
            recv_sem=far_recv.at[part],
            device_id=(to_wave, to_lev),
            device_id_type=MESH,
        )

    def push(start, count, part):
        def one(d, carry):
            far_copy(d, start, count, part).start()
            return carry

        lax.fori_loop(1, DEVICES, one, 0)
        at = pl.multiple_of(pair_of(wave, lev) * PACK + start, 8)
        pltpu.make_async_copy(
            send.at[pl.ds(at, count)], recv.at[me, pl.ds(start, count)], own_sem.at[part]
        ).start()

    def arrive(start, count, part):
        mine = recv.at[me, pl.ds(start, count)]
        pltpu.make_async_copy(mine, mine, own_sem.at[part]).wait()
        block = recv.at[pl.ds(0, DEVICES - 1), pl.ds(start, count)]
        pltpu.make_async_copy(block, block, far_recv.at[part]).wait()

    def left(start, count, part):
        block = recv.at[pl.ds(0, DEVICES - 1), pl.ds(start, count)]
        pltpu.make_async_copy(block, block, far_send.at[part]).wait()

    @pl.when(step == 0)
    def _():
        for g in range(GROUPS, PACK):
            send[pl.ds(g, HALF, stride=PACK), :] = jnp.zeros((HALF, LANES), jnp.float32)

    @pl.when(step == 3)
    def _():
        assemble_pair(0)

    @pl.when(step == STEPS - 1)
    def _():
        assemble_pair(1)
        pl.semaphore_wait(ready, LEVS - 1)
        push(0, FIRST_ROWS, 0)

        count = points_ref[pair_of(wave, lev)]
        points = count.astype(jnp.float32)
        natural = orders_ref[...].reshape(1, M).astype(jnp.float32)
        pieces = [natural[:, w * SLOTS : w * SLOTS + 64] for w in range(WAVES)]
        pieces += [natural[:, w * SLOTS + 64 : (w + 1) * SLOTS] for w in range(WAVES)]
        orders = jnp.concatenate(pieces, axis=1)
        fine_k = lax.broadcasted_iota(jnp.int32, (KBLOCK, 1), 0).astype(jnp.float32)
        fine_c[...], fine_s[...] = turn(fine_k * orders, points)
        coarse_k = lax.broadcasted_iota(jnp.int32, (16, 1), 0).astype(jnp.float32) * KBLOCK
        factor = jnp.where(orders == 0.0, 1.0, 2.0)
        factor = jnp.where(orders <= ((count - 1) // 2).astype(jnp.float32), factor, 0.0)
        whole_c, whole_s = turn(coarse_k * orders, points)
        coarse_c[...] = whole_c * factor
        coarse_s[...] = whole_s * factor

        near_copy(STEPS - 1).wait_recv()

        def one(q, carry):
            assemble(16 + q, lambda u: 64 + 4 * u + q)
            return carry

        lax.fori_loop(0, 4, one, 0)
        push(FIRST_ROWS, LAST_ROWS, 1)

        def basis(a, carry):
            cc, cs = coarse_c[pl.ds(a, 1), :], coarse_s[pl.ds(a, 1), :]
            at = pl.ds(pl.multiple_of(a * KBLOCK, KBLOCK), KBLOCK)
            for lanes in range(0, M, 256):
                part = slice(lanes, lanes + 256)
                fc, fs = fine_c[:, part], fine_s[:, part]
                c, s = cc[:, part], cs[:, part]
                cos_hi[at, part], cos_lo[at, part] = halves(fc * c - fs * s)
                sin_hi[at, part], sin_lo[at, part] = halves(fs * c + fc * s)
            return carry

        lax.fori_loop(0, KBLOCKS, basis, 0)
        parity = (1 - 2 * (orders.astype(jnp.int32) & 1)).astype(jnp.float32)
        for i in range(0, M, LANES):
            wide = jnp.broadcast_to(parity[:, i : i + LANES], (LANES, LANES))
            sign[i : i + LANES, :] = wide.T.astype(jnp.bfloat16)

        lane_block = lax.broadcasted_iota(jnp.int32, (8, LANES), 1) // COLS
        bits = [((lane_block >> t) & 1) == 1 for t in range(3)]

        def spread(w, i0):
            held = [recv[w * LEVS + p, i0 : i0 + 8, :] for p in range(LEVS)]
            for t in range(3):
                held = [jnp.where(bits[t], held[(x + (1 << t)) % 8], held[x]) for x in range(8)]
            for b in range(8):
                moved = held[-b % 8]
                if b:
                    moved = pltpu.roll(moved, LANES - COLS * b, 1)
                u, part = b // 2, b % 2
                if i0 < FIRST_ROWS:
                    base = w * 64 + 4 * i0 + 8 * u
                    coef[part, base : base + 8, :] = moved
                else:
                    base = FIRST + w * 16 + 4 * u
                    coef[part, base : base + 4, :] = moved[:4]

        def split(low, high):
            at = slice(low, high)
            flip_sign = sign[at, :]
            for part, (high_ref, low_ref) in enumerate(((re_hi, re_lo), (im_hi, im_lo))):
                for ref, value in zip((high_ref, low_ref), halves(coef[part, at, :])):
                    ref[at, :LANES] = value
                    ref[at, LANES:] = value * flip_sign

        def partial(rows, cols):
            real = dot(cos_hi[rows, cols], re_hi[cols, :]) + dot(cos_lo[rows, cols], re_hi[cols, :])
            real = real + dot(cos_hi[rows, cols], re_lo[cols, :])
            imag = dot(sin_hi[rows, cols], im_hi[cols, :]) + dot(sin_lo[rows, cols], im_hi[cols, :])
            imag = imag + dot(sin_hi[rows, cols], im_lo[cols, :])
            return real, imag

        arrive(0, FIRST_ROWS, 0)
        for w in range(WAVES):
            for i0 in range(0, FIRST_ROWS, 8):
                spread(w, i0)
        split(0, FIRST)

        def early(a, carry):
            rows = pl.ds(pl.multiple_of(a * KWIDE, 32), KWIDE)
            acc[rows, : 2 * LANES], acc[rows, 2 * LANES :] = partial(rows, slice(0, FIRST))
            return carry

        lax.fori_loop(0, KSPAN // KWIDE, early, 0)

        row = lax.broadcasted_iota(jnp.int32, (64, 4 * LANES), 0)
        col = lax.broadcasted_iota(jnp.int32, (64, 4 * LANES), 1)
        belongs = (
            ((row >> 4) == (col >> 7)) & ((row & 7) == ((col >> 4) & 7)) & (((row >> 3) & 1) == ((col >> 3) & 1))
        )
        gather = jnp.where(belongs, 0.125, 0.0).astype(jnp.bfloat16)
        flip_row = lax.broadcasted_iota(jnp.int32, (LANES, LANES), 0)
        flip_col = lax.broadcasted_iota(jnp.int32, (LANES, LANES), 1)
        flip = jnp.where(flip_row + flip_col == LANES - 1, 1.0, 0.0).astype(jnp.bfloat16)
        quarter = count // 4
        offsets = (0, 2 * quarter - (KSPAN - 1), 2 * quarter, 4 * quarter - (KSPAN - 1))
        shifts = [lax.rem(off + KSPAN, LANES) for off in offsets]
        heads = [(off + KSPAN) // LANES - KBLOCKS for off in offsets]
        shift_bits = [[((shift >> t) & 1) == 1 for t in range(7)] for shift in shifts]

        def turned(tile, x):
            for t in range(7):
                tile = jnp.where(shift_bits[x][t], pltpu.roll(tile, 1 << t, 1), tile)
            return tile


        arrive(FIRST_ROWS, LAST_ROWS, 1)
        for w in range(WAVES):
            spread(w, FIRST_ROWS)
        split(FIRST, M)

        def late(a, carry):
            rows = pl.ds(pl.multiple_of(a * KWIDE, 32), KWIDE)
            real, imag = partial(rows, slice(FIRST, M))
            real, imag = real + acc[rows, : 2 * LANES], imag + acc[rows, 2 * LANES :]
            p, q = real[:, :LANES], real[:, LANES:]
            r, s = imag[:, :LANES], imag[:, LANES:]
            for x, value in enumerate((p - r, q + s, q - s, p + r)):
                part = slice(x * LANES, (x + 1) * LANES)
                sq_hi[rows, part], sq_lo[rows, part] = halves(value * value)
            return carry

        lax.fori_loop(0, KSPAN // KWIDE, late, 0)
        energy = lax.dot_general(gather, sq_hi[...], NT_DIMS, preferred_element_type=jnp.float32)
        energy = energy + lax.dot_general(gather, sq_lo[...], NT_DIMS, preferred_element_type=jnp.float32)
        tiles = [energy[:, a * LANES : (a + 1) * LANES] for a in range(KBLOCKS)]
        for x in (0, 2):
            for a in range(KBLOCKS):
                tile = tiles[a][16 * x : 16 * x + 16]
                cand[x, a] = turned(tile, x) if x else tile
        ahead = jnp.concatenate([tile[16 * x : 16 * x + 16] for x in (1, 3) for tile in reversed(tiles)], axis=0)
        e_hi, e_lo = halves(ahead)
        back = dot(e_hi, flip) + dot(e_lo, flip)
        for x in (1, 3):
            for a in range(KBLOCKS):
                at = (x // 2 * KBLOCKS + a) * 16
                cand[x, a] = turned(back[at : at + 16], x)

        lane = lax.broadcasted_iota(jnp.int32, (16, LANES), 1)

        for t in range(TILES):
            place = t * LANES + lane
            picked = []
            for x in range(4):
                here = jnp.clip(t - heads[x], 0, KBLOCKS - 1)
                before = jnp.clip(t - heads[x] - 1, 0, KBLOCKS - 1)
                picked.append(jnp.where(lane >= shifts[x], cand[x, here], cand[x, before]))
            value = jnp.where(place < count, picked[3], -1.0)
            value = jnp.where(place <= 3 * quarter, picked[2], value)
            value = jnp.where(place <= 2 * quarter, picked[1], value)
            value = jnp.where(place <= quarter, picked[0], value)
            energy_out[pl.ds(t, 16, stride=ROWTILES), :] = value
        for t in range(TILES, ROWTILES):
            energy_out[pl.ds(t, 16, stride=ROWTILES), :] = jnp.zeros((16, LANES), jnp.float32)

        half, band = wave // 8, lax.rem(wave, 8)
        member = half * LEVS + lev

        def rows_of(k):
            return pl.ds(pl.multiple_of(k * ROWTILES, 8), ROWTILES)

        def send_back(d, carry):
            k = lax.rem(member + d, 16)
            pltpu.make_async_remote_copy(
                src_ref=energy_out.at[rows_of(k)],
                dst_ref=got.at[rows_of(member)],
                send_sem=back_send,
                recv_sem=back_recv,
                device_id=(band + 8 * (k // LEVS), lax.rem(k, LEVS)),
                device_id_type=MESH,
            ).start()
            return carry

        lax.fori_loop(1, 16, send_back, 0)
        mine = pltpu.make_async_copy(energy_out.at[rows_of(member)], got.at[rows_of(member)], own_sem.at[0])
        mine.start()
        mine.wait()
        for t in range(STEPS):
            near_copy(t).wait_send()
        left(0, FIRST_ROWS, 0)
        left(FIRST_ROWS, LAST_ROWS, 1)
        part = pl.ds(0, 15 * ROWTILES)
        pltpu.make_async_copy(energy_out.at[part], energy_out.at[part], back_send).wait()
        pltpu.make_async_copy(got.at[part], got.at[part], back_recv).wait()

        for t in range(TILES):
            out_ref[0, :, t * LANES : (t + 1) * LANES] = got[pl.ds(t, 16, stride=ROWTILES), :]


def local(spectral, legendre, wave_map, row_points, brackets, lev_weight, climatology):
    smem = pl.BlockSpec(memory_space=pltpu.SMEM)
    vmem = pl.BlockSpec(memory_space=pltpu.VMEM)
    rows = SLOTS * PER_SLOT
    f32, bf16, dma = jnp.float32, jnp.bfloat16, pltpu.SemaphoreType.DMA
    energy = pl.pallas_call(
        kernel,
        grid=(STEPS,),
        out_shape=jax.ShapeDtypeStruct((1, 16, ROWPAD), f32),
        in_specs=[
            smem,
            smem,
            smem,
            smem,
            vmem,
            pl.BlockSpec((STEP_SLOTS, LEV_DEV * COLS, NT), lambda t: (t, 0, 0)),
            pl.BlockSpec((STEP_SLOTS, HALF, NT), lambda t: (t, 0, 0)),
        ],
        out_specs=vmem,
        scratch_shapes=[
            pltpu.VMEM((rows, HALF), f32),
            pltpu.VMEM((rows, HALF), f32),
            pltpu.VMEM((rows, HALF), f32),
            pltpu.VMEM((HALF * PACK, LANES), f32),
            pltpu.VMEM((DEVICES, PACK, LANES), f32),
            pltpu.VMEM((2, M, LANES), f32),
            pltpu.VMEM((M, LANES), bf16),
            pltpu.VMEM((M, 2 * LANES), bf16),
            pltpu.VMEM((M, 2 * LANES), bf16),
            pltpu.VMEM((M, 2 * LANES), bf16),
            pltpu.VMEM((M, 2 * LANES), bf16),
            pltpu.VMEM((KBLOCK, M), f32),
            pltpu.VMEM((KBLOCK, M), f32),
            pltpu.VMEM((16, M), f32),
            pltpu.VMEM((16, M), f32),
            pltpu.VMEM((KSPAN, M), bf16),
            pltpu.VMEM((KSPAN, M), bf16),
            pltpu.VMEM((KSPAN, M), bf16),
            pltpu.VMEM((KSPAN, M), bf16),
            pltpu.VMEM((KSPAN, 4 * LANES), f32),
            pltpu.VMEM((KSPAN, 4 * LANES), bf16),
            pltpu.VMEM((KSPAN, 4 * LANES), bf16),
            pltpu.VMEM((4, KBLOCKS, 16, LANES), f32),
            pltpu.VMEM((16 * ROWTILES, LANES), f32),
            pltpu.VMEM((16 * ROWTILES, LANES), f32),
            dma((STEPS,)),
            dma((STEPS,)),
            dma((2,)),
            dma((2,)),
            dma((2,)),
            dma,
            dma,
            pltpu.SemaphoreType.REGULAR,
        ],
        compiler_params=pltpu.CompilerParams(
            collective_id=0, has_side_effects=True, vmem_limit_bytes=60 * 1024 * 1024
        ),
        name="transform",
    )(wave_map, brackets, lev_weight, row_points, wave_map, spectral, legendre)
    return jnp.where(energy < 0.0, 0.0, energy - climatology)


def solution(mesh):
    placed = (
        P("wave", "lev", None),
        P("wave", None, None),
        P(),
        P(),
        P(),
        P(),
        P("lev", "wave", None),
    )
    return jax.shard_map(
        local, mesh=mesh, in_specs=placed, out_specs=P("lev", "wave", None), check_vma=False
    )
```

time: 538 us -> 62 us (0.12)
  matrix products: 123 us -> 0 us
  local copies, waits for them, and re-layouts: 119 us -> 0.01 us
  blocking collectives: 103 us -> 0 us
  other arithmetic: 101 us -> 1.74 us
  waiting for transfers between devices: 67.2 us -> 0 us
  Pallas kernels: 0 us -> 60.1 us
  starting transfers between devices: 11.5 us -> 0 us
  loops' own time: 6.9 us -> 0 us
    dot_general x8 -> x0, matrix products: 123 us -> none  [the longest x2 42.2 us: synthesize(): lax.dot_general(ordered[:, :, 1], sine_part, (((0,), (0,)), ((), ())), pr...]
    all_to_all x1 -> x0, blocking collectives: 103 us -> none  [local(): lax.all_to_all(fourier, 'wave', split_axis=2, concat_axis=0, tiled=True)]
    all_to_all x2 -> x0, waiting for transfers between devices: 67.2 us -> none  [the longest x1 60 us: local(): lax.all_to_all(lax.all_to_all(fourier, 'wave', split_axis=2, concat_axis=...]
    scatter x2 -> x0, local copies, waits for them, and re-layouts: 66.2 us -> none  [synthesize(): jnp.zeros_like(coeffs).at[wave_map].set(coeffs) * factor[:, None, None]]
    pallas_call x0 -> x1, Pallas kernels: none -> 60.1 us  [local(): pl.pallas_call(kernel, grid=(STEPS,), out_shape=jax.ShapeDtypeStruct((1,...]
    add x3 -> x0, other arithmetic: 35.9 us -> none  [the longest x2 35.9 us: synthesize(): coarse_sin * fine_cos + coarse_cos * fine_sin]
    sin x2 -> x0, other arithmetic: 35.8 us -> none  [synthesize(): fine_sin = jnp.sin(fine_angle)[None, :, :]]
    all_to_all x4 -> x0, local copies, waits for them, and re-layouts: 24.4 us -> none  [the longest x2 18.9 us: local(): lax.all_to_all(fourier, 'wave', split_axis=2, concat_axis=0, tiled=True)]
  transfers between devices with their start and end apart: 2 -> 0, of which waited for: 2 -> 0; matrix products, arithmetic and copies ran while one was open for 0% -> 0% of each run, Pallas kernels for 0% -> 0%
where the time goes in v2:
time: 62 us; the launch traced here: 61.8 us
  Pallas kernels  60.1 us (97%)
  other arithmetic  1.74 us (3%)
    pallas_call x1, Pallas kernels, local(): pl.pallas_call(kernel, grid=(STEPS,), out_shape=jax.ShapeDtypeStruct((1,...  60.1 us
    select_n x1, other arithmetic, local(): return jnp.where(energy < 0.0, 0.0, energy - climatology)  1.74 us

profile of v2, /device:TPU:1, one launch (start us, length us, event | category | flops | bytes accessed | tf_op | source)
XLA Modules:
  0.0 61.8 jit_solution(15991664465365856330)
XLA Ops:
  0.0 0.0 copy-start
  0.0 60.1 %transform.1 = f32[1,16,5248]{2,1,0:T(8,128)} custom-call(s32[1280]{0:T(1024)} %orders_ref.1, s32[8]{0:T(128)} %brackets_ref.1, f32[8]{0:T(128)} %weight_ref.1, s32[128]{0:T(128)} %points_ref.1, s32[1280]{0:T(1024)} %orders_ref.1, bf16[80,64,1280]{2,1,0:T(8,128)(2,1)} %spec_ref.1, bf16[80,128,1280]{2,1,0:T(8,128)(2,1)} %leg_ref.1), custom_call_target="tpu_custom_call" | custom-call | tf_op jit(solution)/shard_map/transform/pallas_call | solution.py:413
  60.1 0.0 copy-done
  60.1 1.7 %subtract_select_fusion = f32[1,16,5248]{2,1,0:T(8,128)} fusion(f32[1,16,5248]{2,1,0:T(8,128)} %transform.1, f32[1,16,5248]{2,1,0:T(8,128)S(1)} %copy-done), kind=kLoop, calls=%fused_computation | loop fusion | flops 251904 | bytes 1007616 | tf_op jit(solution)/shard_map/jit(_where)/select_n | solution.py:467
Async XLA Ops:
  0.0 60.1 %copy-start = (f32[1,16,5248]{2,1,0:T(8,128)S(1)}, f32[1,16,5248]{2,1,0:T(8,128)}, u32[]{:S(2)}) copy-start(f32[1,16,5248]{2,1,0:T(8,128)} %param.13) | copy-start | bytes 1007620

commit v3 on v2

--- a/solution.py
+++ b/solution.py
@@ -22,15 +22,16 @@
 LEVS = 8
 DEVICES = WAVES * LEVS
 SLOTS = M // WAVES
-STEP_SLOTS = 16
+STEP_SLOTS = 8
 STEPS = SLOTS // STEP_SLOTS
 STEP_ROWS = STEP_SLOTS * 2 * COLS
 PER_SLOT = 2 * COLS
-FIRST_ROWS, LAST_ROWS = 16, 8
-PACK = FIRST_ROWS + LAST_ROWS
 GROUPS = SLOTS // 4
-FIRST = WAVES * 64
-LAST = WAVES * 16
+PARTS = ((0, 32, 8), (32, 32, 8), (64, 16, 4))
+PACK = 2 * GROUPS
+PART_AT = (0, 16, 32)
+PART_SLOT = (0, WAVES * 32, WAVES * 64)
+BUFFERS = 4
 STRIDE = 37
 
 KBLOCK = 128
@@ -73,16 +74,34 @@
 
 
 def kernel(
-    waves_ref, brackets_ref, weight_ref, points_ref, orders_ref, spec_ref, leg_ref, out_ref,
-    mixed, first, other, send, recv, coef, sign, re_hi, re_lo, im_hi, im_lo,
+    waves_ref, brackets_ref, weight_ref, points_ref, orders_ref, spec_hbm, leg_hbm, out_ref,
+    spec_ref, leg_ref, load_sem, mixed, first, other, send, recv, coef, sign, re_hi, re_lo, im_hi, im_lo,
     fine_c, fine_s, coarse_c, coarse_s, cos_hi, cos_lo, sin_hi, sin_lo, acc, sq_hi, sq_lo, cand, energy_out, got,
     near_send, near_recv, far_send, far_recv, own_sem, back_send, back_recv, ready,
 ):
     step = pl.program_id(0)
     wave, lev = lax.axis_index("wave"), lax.axis_index("lev")
     me = wave * LEVS + lev
-    below = lax.rem(lev + LEVS - 1, LEVS)
     barrier = pltpu.get_barrier_semaphore()
+
+    def loads(t):
+        slot = lax.rem(t, BUFFERS)
+        at = pl.ds(pl.multiple_of(t * STEP_SLOTS, STEP_SLOTS), STEP_SLOTS)
+        return (
+            pltpu.make_async_copy(spec_hbm.at[at], spec_ref.at[slot], load_sem.at[0, slot]),
+            pltpu.make_async_copy(leg_hbm.at[at], leg_ref.at[slot], load_sem.at[1, slot]),
+        )
+
+    @pl.when(step == 0)
+    def _():
+        for t in range(BUFFERS - 1):
+            for load in loads(t):
+                load.start()
+
+    @pl.when(step + BUFFERS - 1 < STEPS)
+    def _():
+        for load in loads(step + BUFFERS - 1):
+            load.start()
 
     @pl.when(step == 0)
     def _():
@@ -97,21 +116,155 @@
 
     lower = brackets_ref[lev] - lev * LEV_DEV
     weight = weight_ref[lev]
-    inside = lower < LEV_DEV - 1
-    gain = jnp.where(inside, 0.0, 1.0 - weight)
+    gain = jnp.where(lower == LEV_DEV - 1, 1.0 - weight, 0.0)
+    odd = (lev & 1) == 1
+    even = (lev & 1) == 0
+    prior = jnp.maximum(lev - 1, 0)
+    prior_last = (brackets_ref[prior] == prior * LEV_DEV + LEV_DEV - 1) & (lev > 0)
+    prior_gain = jnp.where(prior_last, 1.0 - weight_ref[prior], 0.0)
     level_weight = [
         jnp.where(lower == v, weight, 0.0) + jnp.where(lower + 1 == v, 1.0 - weight, 0.0) for v in range(LEV_DEV)
     ]
 
+    def near_copy(t):
+        rows = pl.ds(pl.multiple_of(t * STEP_ROWS, STEP_ROWS), STEP_ROWS)
+        return pltpu.make_async_remote_copy(
+            src_ref=first.at[rows],
+            dst_ref=other.at[rows],
+            send_sem=near_send.at[t],
+            recv_sem=near_recv.at[t],
+            device_id=(wave, lev ^ 1),
+            device_id_type=MESH,
+        )
+
+    def assemble(g, slot_of, turn_by, value, row):
+        pieces = []
+        for c in range(8):
+            b = (c - turn_by + 8) & 7
+            base = slot_of(b >> 1) * PER_SLOT + (b & 1)
+            for hemi in range(2):
+                pieces.append(value(pl.ds(base + hemi * COLS, 8, stride=2)))
+        send[pl.ds(row, HALF, stride=PACK), :] = jnp.concatenate(pieces, axis=0).T
+
+    def assemble_part(part):
+        begin, slots, count = PARTS[part]
+        at = PART_AT[part]
+
+        @pl.when(even)
+        def _():
+            for t in range(begin // STEP_SLOTS, (begin + slots) // STEP_SLOTS):
+                near_copy(t).wait_recv()
+
+            def one(r, carry):
+                slot_of = lambda u: begin + count * u + r
+                assemble(r, slot_of, lev, lambda rows: mixed[rows, :] + gain * other[rows, :], at + r)
+                assemble(r, slot_of, lev - 1, lambda rows: prior_gain * first[rows, :], at + count + r)
+                return carry
+
+            lax.fori_loop(0, count, one, 0)
+
+        @pl.when(odd)
+        def _():
+            def one(r, carry):
+                assemble(r, lambda u: begin + count * u + r, lev, lambda rows: mixed[rows, :], at + r)
+                return carry
+
+            lax.fori_loop(0, count, one, 0)
+
+    def push(part):
+        at, count = PART_AT[part], PARTS[part][2]
+
+        def send_rows(height):
+            def one(i, carry):
+                d = (STRIDE * i) & (DEVICES - 1)
+                dw, dl = d >> 3, d & 7
+                pair = pair_of(wave, lev) ^ (((dw & 7) << 4) | ((dw >> 3) << 3) | dl)
+                pltpu.make_async_remote_copy(
+                    src_ref=send.at[pl.ds(pl.multiple_of(pair * PACK + at, 8), height)],
+                    dst_ref=recv.at[pl.ds(pl.multiple_of(me * PACK + at, 8), height)],
+                    send_sem=far_send.at[part],
+                    recv_sem=far_recv.at[part],
+                    device_id=(wave ^ dw, lev ^ dl),
+                    device_id_type=MESH,
+                ).start()
+                return carry
+
+            lax.fori_loop(1, DEVICES, one, 0)
+
+        if count == 8:
+            pl.when(even)(lambda: send_rows(16))
+            pl.when(odd)(lambda: send_rows(8))
+        else:
+            send_rows(8)
+        mine = pl.multiple_of(pair_of(wave, lev) * PACK + at, 8)
+        pltpu.make_async_copy(
+            send.at[pl.ds(mine, 2 * count)],
+            recv.at[pl.ds(pl.multiple_of(me * PACK + at, 8), 2 * count)],
+            own_sem.at[part],
+        ).start()
+
+    def all_of(part, sem, even_rows, odd_rows):
+        def wait(rows):
+            block = recv.at[pl.ds(0, rows)]
+            pltpu.make_async_copy(block, block, sem.at[part]).wait()
+
+        if PARTS[part][2] == 8:
+            pl.when(even)(lambda: wait(even_rows))
+            pl.when(odd)(lambda: wait(odd_rows))
+        else:
+            wait((DEVICES - 1) * 8)
+
+    def arrive(part):
+        mine = recv.at[pl.ds(0, 2 * PARTS[part][2])]
+        pltpu.make_async_copy(mine, mine, own_sem.at[part]).wait()
+        others = DEVICES // 2
+        all_of(part, far_recv, (others - 1) * 16 + others * 8, others * 16 + (others - 1) * 8)
+
+    def left(part):
+        all_of(part, far_send, (DEVICES - 1) * 16, (DEVICES - 1) * 8)
+
+    @pl.when(step == 1)
+    def _():
+        pl.semaphore_wait(barrier, LEVS + WAVES - 2)
+        for d in range(1, LEVS):
+            pl.semaphore_signal(
+                ready, inc=1, device_id=(wave, lax.rem(lev + d, LEVS)), device_id_type=MESH
+            )
+
+        @pl.when(odd)
+        def _():
+            near_copy(0).start()
+
+    @pl.when(step == 0)
+    def _():
+        for part in range(3):
+            _, _, count = PARTS[part]
+            for r in range(count):
+                send[pl.ds(PART_AT[part] + count + r, HALF, stride=PACK), :] = jnp.zeros((HALF, LANES), jnp.float32)
+
+    @pl.when(step == 4)
+    def _():
+        assemble_part(0)
+        pl.semaphore_wait(ready, LEVS - 1)
+        push(0)
+
+    @pl.when(step == STEPS - 1)
+    def _():
+        assemble_part(1)
+        push(1)
+
+    for load in loads(step):
+        load.wait()
+    held_at = lax.rem(step, BUFFERS)
     degree = lax.broadcasted_iota(jnp.int32, (1, NT), 1)
     for i in range(STEP_SLOTS):
         order = waves_ref[wave * SLOTS + step * STEP_SLOTS + i]
         kept = jnp.where(degree >= order, 1.0, 0.0)
         signed = kept * (1 - 2 * ((degree + order) & 1)).astype(jnp.float32)
         kept, signed = kept.astype(jnp.bfloat16), signed.astype(jnp.bfloat16)
-        coeffs = spec_ref[i]
+        coeffs = spec_ref[held_at, i]
         both = jnp.concatenate([coeffs * kept, coeffs * signed], axis=0)
-        sums = lax.dot_general(both, leg_ref[i], NT_DIMS, preferred_element_type=jnp.float32)
+        sums = lax.dot_general(both, leg_ref[held_at, i], NT_DIMS, preferred_element_type=jnp.float32)
         base = step * STEP_ROWS + i * PER_SLOT
         for hemi in range(2):
             own = [sums[(LEV_DEV * hemi + v) * COLS : (LEV_DEV * hemi + v + 1) * COLS] for v in range(LEV_DEV)]
@@ -122,102 +275,21 @@
             mixed[at, :] = total
             first[at, :] = own[0]
 
-    def near_copy(t):
-        rows = pl.ds(pl.multiple_of(t * STEP_ROWS, STEP_ROWS), STEP_ROWS)
-        return pltpu.make_async_remote_copy(
-            src_ref=first.at[rows],
-            dst_ref=other.at[rows],
-            send_sem=near_send.at[t],
-            recv_sem=near_recv.at[t],
-            device_id=(wave, below),
-            device_id_type=MESH,
-        )
-
-    @pl.when(step == 0)
-    def _():
-        pl.semaphore_wait(barrier, LEVS + WAVES - 2)
-        for d in range(1, LEVS):
-            pl.semaphore_signal(
-                ready, inc=1, device_id=(wave, lax.rem(lev + d, LEVS)), device_id_type=MESH
-            )
-
-    near_copy(step).start()
-
-    def assemble(g, slot_of):
-        pieces = []
-        for c in range(8):
-            b = lax.rem(c - lev + 8, 8)
-            base = slot_of(b // 2) * PER_SLOT + lax.rem(b, 2)
-            for hemi in range(2):
-                at = pl.ds(base + hemi * COLS, 8, stride=2)
-                pieces.append(mixed[at, :] + gain * other[at, :])
-        block = jnp.concatenate(pieces, axis=0)
-        send[pl.ds(g, HALF, stride=PACK), :] = block.T
-
-    def assemble_pair(tau):
-        near_copy(2 * tau).wait_recv()
-        near_copy(2 * tau + 1).wait_recv()
-
-        def one(r, carry):
-            assemble(8 * tau + r, lambda u: 32 * tau + 8 * u + r)
-            return carry
-
-        lax.fori_loop(0, 8, one, 0)
-
-    def far_copy(d, start, count, part):
-        target = lax.rem(me + STRIDE * d, DEVICES)
-        to_wave, to_lev = target // LEVS, lax.rem(target, LEVS)
-        at = pl.multiple_of(pair_of(to_wave, to_lev) * PACK + start, 8)
-        return pltpu.make_async_remote_copy(
-            src_ref=send.at[pl.ds(at, count)],
-            dst_ref=recv.at[me, pl.ds(start, count)],
-            send_sem=far_send.at[part],
-            recv_sem=far_recv.at[part],
-            device_id=(to_wave, to_lev),
-            device_id_type=MESH,
-        )
-
-    def push(start, count, part):
-        def one(d, carry):
-            far_copy(d, start, count, part).start()
-            return carry
-
-        lax.fori_loop(1, DEVICES, one, 0)
-        at = pl.multiple_of(pair_of(wave, lev) * PACK + start, 8)
-        pltpu.make_async_copy(
-            send.at[pl.ds(at, count)], recv.at[me, pl.ds(start, count)], own_sem.at[part]
-        ).start()
-
-    def arrive(start, count, part):
-        mine = recv.at[me, pl.ds(start, count)]
-        pltpu.make_async_copy(mine, mine, own_sem.at[part]).wait()
-        block = recv.at[pl.ds(0, DEVICES - 1), pl.ds(start, count)]
-        pltpu.make_async_copy(block, block, far_recv.at[part]).wait()
-
-    def left(start, count, part):
-        block = recv.at[pl.ds(0, DEVICES - 1), pl.ds(start, count)]
-        pltpu.make_async_copy(block, block, far_send.at[part]).wait()
-
-    @pl.when(step == 0)
-    def _():
-        for g in range(GROUPS, PACK):
-            send[pl.ds(g, HALF, stride=PACK), :] = jnp.zeros((HALF, LANES), jnp.float32)
-
-    @pl.when(step == 3)
-    def _():
-        assemble_pair(0)
+    @pl.when(odd & (step > 0))
+    def _():
+        near_copy(step).start()
 
     @pl.when(step == STEPS - 1)
     def _():
-        assemble_pair(1)
-        pl.semaphore_wait(ready, LEVS - 1)
-        push(0, FIRST_ROWS, 0)
+        assemble_part(2)
+        push(2)
 
         count = points_ref[pair_of(wave, lev)]
         points = count.astype(jnp.float32)
         natural = orders_ref[...].reshape(1, M).astype(jnp.float32)
-        pieces = [natural[:, w * SLOTS : w * SLOTS + 64] for w in range(WAVES)]
-        pieces += [natural[:, w * SLOTS + 64 : (w + 1) * SLOTS] for w in range(WAVES)]
+        pieces = []
+        for begin, slots, _ in PARTS:
+            pieces += [natural[:, w * SLOTS + begin : w * SLOTS + begin + slots] for w in range(WAVES)]
         orders = jnp.concatenate(pieces, axis=1)
         fine_k = lax.broadcasted_iota(jnp.int32, (KBLOCK, 1), 0).astype(jnp.float32)
         fine_c[...], fine_s[...] = turn(fine_k * orders, points)
@@ -227,15 +299,6 @@
         whole_c, whole_s = turn(coarse_k * orders, points)
         coarse_c[...] = whole_c * factor
         coarse_s[...] = whole_s * factor
-
-        near_copy(STEPS - 1).wait_recv()
-
-        def one(q, carry):
-            assemble(16 + q, lambda u: 64 + 4 * u + q)
-            return carry
-
-        lax.fori_loop(0, 4, one, 0)
-        push(FIRST_ROWS, LAST_ROWS, 1)
 
         def basis(a, carry):
             cc, cs = coarse_c[pl.ds(a, 1), :], coarse_s[pl.ds(a, 1), :]
@@ -257,21 +320,23 @@
         lane_block = lax.broadcasted_iota(jnp.int32, (8, LANES), 1) // COLS
         bits = [((lane_block >> t) & 1) == 1 for t in range(3)]
 
-        def spread(w, i0):
-            held = [recv[w * LEVS + p, i0 : i0 + 8, :] for p in range(LEVS)]
+        def spread(w, part):
+            _, slots, count = PARTS[part]
+            at = [(w * LEVS + p) * PACK + PART_AT[part] for p in range(LEVS)]
+            held = [recv[at[p] : at[p] + 8, :] for p in range(LEVS)]
+            for p in range(1, LEVS - 1, 2):
+                if count == 8:
+                    held[p] = held[p] + recv[at[p + 1] + 8 : at[p + 1] + 16, :]
+                else:
+                    held[p] = held[p] + pltpu.roll(held[p + 1], 4, 0)
             for t in range(3):
                 held = [jnp.where(bits[t], held[(x + (1 << t)) % 8], held[x]) for x in range(8)]
             for b in range(8):
                 moved = held[-b % 8]
                 if b:
                     moved = pltpu.roll(moved, LANES - COLS * b, 1)
-                u, part = b // 2, b % 2
-                if i0 < FIRST_ROWS:
-                    base = w * 64 + 4 * i0 + 8 * u
-                    coef[part, base : base + 8, :] = moved
-                else:
-                    base = FIRST + w * 16 + 4 * u
-                    coef[part, base : base + 4, :] = moved[:4]
+                base = PART_SLOT[part] + w * slots + count * (b // 2)
+                coef[b % 2, base : base + count, :] = moved[:count]
 
         def split(low, high):
             at = slice(low, high)
@@ -288,18 +353,32 @@
             imag = imag + dot(sin_hi[rows, cols], im_lo[cols, :])
             return real, imag
 
-        arrive(0, FIRST_ROWS, 0)
-        for w in range(WAVES):
-            for i0 in range(0, FIRST_ROWS, 8):
-                spread(w, i0)
-        split(0, FIRST)
+        def gathered(part):
+            arrive(part)
+            for w in range(WAVES):
+                spread(w, part)
+            begin = PART_SLOT[part]
+            split(begin, begin + WAVES * PARTS[part][1])
+            return slice(begin, begin + WAVES * PARTS[part][1])
+
+        cols = gathered(0)
 
         def early(a, carry):
             rows = pl.ds(pl.multiple_of(a * KWIDE, 32), KWIDE)
-            acc[rows, : 2 * LANES], acc[rows, 2 * LANES :] = partial(rows, slice(0, FIRST))
+            acc[rows, : 2 * LANES], acc[rows, 2 * LANES :] = partial(rows, cols)
             return carry
 
         lax.fori_loop(0, KSPAN // KWIDE, early, 0)
+        cols_next = gathered(1)
+
+        def second(a, carry):
+            rows = pl.ds(pl.multiple_of(a * KWIDE, 32), KWIDE)
+            real, imag = partial(rows, cols_next)
+            acc[rows, : 2 * LANES] = acc[rows, : 2 * LANES] + real
+            acc[rows, 2 * LANES :] = acc[rows, 2 * LANES :] + imag
+            return carry
+
+        lax.fori_loop(0, KSPAN // KWIDE, second, 0)
 
         row = lax.broadcasted_iota(jnp.int32, (64, 4 * LANES), 0)
         col = lax.broadcasted_iota(jnp.int32, (64, 4 * LANES), 1)
@@ -322,14 +401,11 @@
             return tile
 
 
-        arrive(FIRST_ROWS, LAST_ROWS, 1)
-        for w in range(WAVES):
-            spread(w, FIRST_ROWS)
-        split(FIRST, M)
+        cols_last = gathered(2)
 
         def late(a, carry):
             rows = pl.ds(pl.multiple_of(a * KWIDE, 32), KWIDE)
-            real, imag = partial(rows, slice(FIRST, M))
+            real, imag = partial(rows, cols_last)
             real, imag = real + acc[rows, : 2 * LANES], imag + acc[rows, 2 * LANES :]
             p, q = real[:, :LANES], real[:, LANES:]
             r, s = imag[:, :LANES], imag[:, LANES:]
@@ -378,13 +454,13 @@
             return pl.ds(pl.multiple_of(k * ROWTILES, 8), ROWTILES)
 
         def send_back(d, carry):
-            k = lax.rem(member + d, 16)
+            k = member ^ d
             pltpu.make_async_remote_copy(
                 src_ref=energy_out.at[rows_of(k)],
                 dst_ref=got.at[rows_of(member)],
                 send_sem=back_send,
                 recv_sem=back_recv,
-                device_id=(band + 8 * (k // LEVS), lax.rem(k, LEVS)),
+                device_id=(band + 8 * (k >> 3), k & 7),
                 device_id_type=MESH,
             ).start()
             return carry
@@ -393,10 +469,14 @@
         mine = pltpu.make_async_copy(energy_out.at[rows_of(member)], got.at[rows_of(member)], own_sem.at[0])
         mine.start()
         mine.wait()
-        for t in range(STEPS):
-            near_copy(t).wait_send()
-        left(0, FIRST_ROWS, 0)
-        left(FIRST_ROWS, LAST_ROWS, 1)
+
+        @pl.when(odd)
+        def _():
+            for t in range(STEPS):
+                near_copy(t).wait_send()
+
+        for part in range(3):
+            left(part)
         part = pl.ds(0, 15 * ROWTILES)
         pltpu.make_async_copy(energy_out.at[part], energy_out.at[part], back_send).wait()
         pltpu.make_async_copy(got.at[part], got.at[part], back_recv).wait()
@@ -408,6 +488,7 @@
 def local(spectral, legendre, wave_map, row_points, brackets, lev_weight, climatology):
     smem = pl.BlockSpec(memory_space=pltpu.SMEM)
     vmem = pl.BlockSpec(memory_space=pltpu.VMEM)
+    hbm = pl.BlockSpec(memory_space=pl.ANY)
     rows = SLOTS * PER_SLOT
     f32, bf16, dma = jnp.float32, jnp.bfloat16, pltpu.SemaphoreType.DMA
     energy = pl.pallas_call(
@@ -420,16 +501,19 @@
             smem,
             smem,
             vmem,
-            pl.BlockSpec((STEP_SLOTS, LEV_DEV * COLS, NT), lambda t: (t, 0, 0)),
-            pl.BlockSpec((STEP_SLOTS, HALF, NT), lambda t: (t, 0, 0)),
+            hbm,
+            hbm,
         ],
         out_specs=vmem,
         scratch_shapes=[
+            pltpu.VMEM((BUFFERS, STEP_SLOTS, LEV_DEV * COLS, NT), bf16),
+            pltpu.VMEM((BUFFERS, STEP_SLOTS, HALF, NT), bf16),
+            dma((2, BUFFERS)),
             pltpu.VMEM((rows, HALF), f32),
             pltpu.VMEM((rows, HALF), f32),
             pltpu.VMEM((rows, HALF), f32),
             pltpu.VMEM((HALF * PACK, LANES), f32),
-            pltpu.VMEM((DEVICES, PACK, LANES), f32),
+            pltpu.VMEM((DEVICES * PACK, LANES), f32),
             pltpu.VMEM((2, M, LANES), f32),
             pltpu.VMEM((M, LANES), bf16),
             pltpu.VMEM((M, 2 * LANES), bf16),
@@ -452,15 +536,15 @@
             pltpu.VMEM((16 * ROWTILES, LANES), f32),
             dma((STEPS,)),
             dma((STEPS,)),
-            dma((2,)),
-            dma((2,)),
-            dma((2,)),
+            dma((3,)),
+            dma((3,)),
+            dma((3,)),
             dma,
             dma,
             pltpu.SemaphoreType.REGULAR,
         ],
         compiler_params=pltpu.CompilerParams(
-            collective_id=0, has_side_effects=True, vmem_limit_bytes=60 * 1024 * 1024
+            collective_id=0, has_side_effects=True, vmem_limit_bytes=58 * 1024 * 1024
         ),
         name="transform",
     )(wave_map, brackets, lev_weight, row_points, wave_map, spectral, legendre)

time: 62 us -> 56.3 us (0.908)
  Pallas kernels: 60.1 us -> 54.3 us
    pallas_call x1, Pallas kernels: 60.1 us -> 54.3 us  [local(): pl.pallas_call(kernel, grid=(STEPS,), out_shape=jax.ShapeDtypeStruct((1,...]
where the time goes in v3:
time: 56.3 us; the launch traced here: 56.1 us
  Pallas kernels  54.3 us (96%)
  other arithmetic  1.74 us (3%)
    pallas_call x1, Pallas kernels, local(): pl.pallas_call(kernel, grid=(STEPS,), out_shape=jax.ShapeDtypeStruct((1,...  54.3 us
    select_n x1, other arithmetic, local(): return jnp.where(energy < 0.0, 0.0, energy - climatology)  1.74 us

profile of v3, /device:TPU:1, one launch (start us, length us, event | category | flops | bytes accessed | tf_op | source)
XLA Modules:
  0.0 56.1 jit_solution(5206183009074623892)
XLA Ops:
  0.0 0.0 copy-start
  0.0 54.3 %transform.1 = f32[1,16,5248]{2,1,0:T(8,128)} custom-call(s32[1280]{0:T(1024)} %orders_ref.1, s32[8]{0:T(128)} %brackets_ref.1, f32[8]{0:T(128)} %weight_ref.1, s32[128]{0:T(128)} %points_ref.1, s32[1280]{0:T(1024)} %orders_ref.1, bf16[80,64,1280]{2,1,0:T(8,128)(2,1)} %spec_hbm.1, bf16[80,128,1280]{2,1,0:T(8,128)(2,1)} %leg_hbm.1), custom_call_target="tpu_custom_call" | custom-call | tf_op jit(solution)/shard_map/transform/pallas_call | solution.py:494
  54.4 0.0 copy-done
  54.4 1.7 %subtract_select_fusion = f32[1,16,5248]{2,1,0:T(8,128)} fusion(f32[1,16,5248]{2,1,0:T(8,128)} %transform.1, f32[1,16,5248]{2,1,0:T(8,128)S(1)} %copy-done), kind=kLoop, calls=%fused_computation | loop fusion | flops 251904 | bytes 1007616 | tf_op jit(solution)/shard_map/jit(_where)/select_n | solution.py:551
Async XLA Ops:
  0.0 54.4 %copy-start = (f32[1,16,5248]{2,1,0:T(8,128)S(1)}, f32[1,16,5248]{2,1,0:T(8,128)}, u32[]{:S(2)}) copy-start(f32[1,16,5248]{2,1,0:T(8,128)} %param.13) | copy-start | bytes 1007620

commit v4 on v3

--- a/solution.py
+++ b/solution.py
@@ -37,7 +37,8 @@
 KBLOCK = 128
 KBLOCKS = 11
 KSPAN = KBLOCK * KBLOCKS
-KWIDE = 352
+KWIDE = 432
+KUSED = 3 * KWIDE
 TILES = ROWPAD // LANES
 ROWTILES = 48
 
@@ -74,8 +75,8 @@
 
 
 def kernel(
-    waves_ref, brackets_ref, weight_ref, points_ref, orders_ref, spec_hbm, leg_hbm, out_ref,
-    spec_ref, leg_ref, load_sem, mixed, first, other, send, recv, coef, sign, re_hi, re_lo, im_hi, im_lo,
+    waves_hbm, brackets_hbm, weight_hbm, points_hbm, spec_hbm, leg_hbm, out_ref,
+    waves_ref, brackets_ref, weight_ref, points_ref, orders_ref, small_sem, spec_ref, leg_ref, load_sem, mixed, first, other, send, recv, coef, sign, re_hi, re_lo, im_hi, im_lo,
     fine_c, fine_s, coarse_c, coarse_s, cos_hi, cos_lo, sin_hi, sin_lo, acc, sq_hi, sq_lo, cand, energy_out, got,
     near_send, near_recv, far_send, far_recv, own_sem, back_send, back_recv, ready,
 ):
@@ -92,8 +93,23 @@
             pltpu.make_async_copy(leg_hbm.at[at], leg_ref.at[slot], load_sem.at[1, slot]),
         )
 
+    smalls = [
+        pltpu.make_async_copy(source, target, small_sem.at[i])
+        for i, (source, target) in enumerate(
+            (
+                (brackets_hbm, brackets_ref),
+                (weight_hbm, weight_ref),
+                (waves_hbm, waves_ref),
+                (points_hbm, points_ref),
+                (waves_hbm, orders_ref),
+            )
+        )
+    ]
+
     @pl.when(step == 0)
     def _():
+        for small in smalls:
+            small.start()
         for t in range(BUFFERS - 1):
             for load in loads(t):
                 load.start()
@@ -114,11 +130,18 @@
                 barrier, inc=1, device_id=(lax.rem(wave + d, WAVES), lev), device_id_type=MESH
             )
 
+    @pl.when(step == 0)
+    def _():
+        for small in smalls:
+            small.wait()
+
     lower = brackets_ref[lev] - lev * LEV_DEV
     weight = weight_ref[lev]
     gain = jnp.where(lower == LEV_DEV - 1, 1.0 - weight, 0.0)
     odd = (lev & 1) == 1
     even = (lev & 1) == 0
+    wide = even & (lev > 0)
+    narrow = odd | (lev == 0)
     prior = jnp.maximum(lev - 1, 0)
     prior_last = (brackets_ref[prior] == prior * LEV_DEV + LEV_DEV - 1) & (lev > 0)
     prior_gain = jnp.where(prior_last, 1.0 - weight_ref[prior], 0.0)
@@ -192,8 +215,8 @@
             lax.fori_loop(1, DEVICES, one, 0)
 
         if count == 8:
-            pl.when(even)(lambda: send_rows(16))
-            pl.when(odd)(lambda: send_rows(8))
+            pl.when(wide)(lambda: send_rows(16))
+            pl.when(narrow)(lambda: send_rows(8))
         else:
             send_rows(8)
         mine = pl.multiple_of(pair_of(wave, lev) * PACK + at, 8)
@@ -203,27 +226,28 @@
             own_sem.at[part],
         ).start()
 
-    def all_of(part, sem, even_rows, odd_rows):
+    def all_of(part, sem, wide_rows, narrow_rows):
         def wait(rows):
             block = recv.at[pl.ds(0, rows)]
             pltpu.make_async_copy(block, block, sem.at[part]).wait()
 
         if PARTS[part][2] == 8:
-            pl.when(even)(lambda: wait(even_rows))
-            pl.when(odd)(lambda: wait(odd_rows))
+            pl.when(wide)(lambda: wait(wide_rows))
+            pl.when(narrow)(lambda: wait(narrow_rows))
         else:
             wait((DEVICES - 1) * 8)
 
     def arrive(part):
         mine = recv.at[pl.ds(0, 2 * PARTS[part][2])]
         pltpu.make_async_copy(mine, mine, own_sem.at[part]).wait()
-        others = DEVICES // 2
-        all_of(part, far_recv, (others - 1) * 16 + others * 8, others * 16 + (others - 1) * 8)
+        wides = WAVES * (LEVS // 2 - 1)
+        total = wides * 16 + (DEVICES - wides) * 8
+        all_of(part, far_recv, total - 16, total - 8)
 
     def left(part):
         all_of(part, far_send, (DEVICES - 1) * 16, (DEVICES - 1) * 8)
 
-    @pl.when(step == 1)
+    @pl.when(step == 2)
     def _():
         pl.semaphore_wait(barrier, LEVS + WAVES - 2)
         for d in range(1, LEVS):
@@ -234,6 +258,7 @@
         @pl.when(odd)
         def _():
             near_copy(0).start()
+            near_copy(1).start()
 
     @pl.when(step == 0)
     def _():
@@ -275,7 +300,7 @@
             mixed[at, :] = total
             first[at, :] = own[0]
 
-    @pl.when(odd & (step > 0))
+    @pl.when(odd & (step > 1))
     def _():
         near_copy(step).start()
 
@@ -364,21 +389,21 @@
         cols = gathered(0)
 
         def early(a, carry):
-            rows = pl.ds(pl.multiple_of(a * KWIDE, 32), KWIDE)
+            rows = pl.ds(pl.multiple_of(a * KWIDE, 16), KWIDE)
             acc[rows, : 2 * LANES], acc[rows, 2 * LANES :] = partial(rows, cols)
             return carry
 
-        lax.fori_loop(0, KSPAN // KWIDE, early, 0)
+        lax.fori_loop(0, KUSED // KWIDE, early, 0)
         cols_next = gathered(1)
 
         def second(a, carry):
-            rows = pl.ds(pl.multiple_of(a * KWIDE, 32), KWIDE)
+            rows = pl.ds(pl.multiple_of(a * KWIDE, 16), KWIDE)
             real, imag = partial(rows, cols_next)
             acc[rows, : 2 * LANES] = acc[rows, : 2 * LANES] + real
             acc[rows, 2 * LANES :] = acc[rows, 2 * LANES :] + imag
             return carry
 
-        lax.fori_loop(0, KSPAN // KWIDE, second, 0)
+        lax.fori_loop(0, KUSED // KWIDE, second, 0)
 
         row = lax.broadcasted_iota(jnp.int32, (64, 4 * LANES), 0)
         col = lax.broadcasted_iota(jnp.int32, (64, 4 * LANES), 1)
@@ -386,25 +411,23 @@
             ((row >> 4) == (col >> 7)) & ((row & 7) == ((col >> 4) & 7)) & (((row >> 3) & 1) == ((col >> 3) & 1))
         )
         gather = jnp.where(belongs, 0.125, 0.0).astype(jnp.bfloat16)
-        flip_row = lax.broadcasted_iota(jnp.int32, (LANES, LANES), 0)
-        flip_col = lax.broadcasted_iota(jnp.int32, (LANES, LANES), 1)
-        flip = jnp.where(flip_row + flip_col == LANES - 1, 1.0, 0.0).astype(jnp.bfloat16)
         quarter = count // 4
         offsets = (0, 2 * quarter - (KSPAN - 1), 2 * quarter, 4 * quarter - (KSPAN - 1))
         shifts = [lax.rem(off + KSPAN, LANES) for off in offsets]
         heads = [(off + KSPAN) // LANES - KBLOCKS for off in offsets]
-        shift_bits = [[((shift >> t) & 1) == 1 for t in range(7)] for shift in shifts]
-
-        def turned(tile, x):
-            for t in range(7):
-                tile = jnp.where(shift_bits[x][t], pltpu.roll(tile, 1 << t, 1), tile)
-            return tile
-
+        old = lax.broadcasted_iota(jnp.int32, (LANES, LANES), 0)
+        new = lax.broadcasted_iota(jnp.int32, (LANES, LANES), 1)
+        places = [None] + [
+            jnp.where((((LANES - 1 - old) if x % 2 else old) + shifts[x]) & (LANES - 1) == new, 1.0, 0.0)
+            for x in (1, 2, 3)
+        ]
+        sq_hi[KUSED:, :] = jnp.zeros((KSPAN - KUSED, 4 * LANES), jnp.bfloat16)
+        sq_lo[KUSED:, :] = jnp.zeros((KSPAN - KUSED, 4 * LANES), jnp.bfloat16)
 
         cols_last = gathered(2)
 
         def late(a, carry):
-            rows = pl.ds(pl.multiple_of(a * KWIDE, 32), KWIDE)
+            rows = pl.ds(pl.multiple_of(a * KWIDE, 16), KWIDE)
             real, imag = partial(rows, cols_last)
             real, imag = real + acc[rows, : 2 * LANES], imag + acc[rows, 2 * LANES :]
             p, q = real[:, :LANES], real[:, LANES:]
@@ -414,25 +437,23 @@
                 sq_hi[rows, part], sq_lo[rows, part] = halves(value * value)
             return carry
 
-        lax.fori_loop(0, KSPAN // KWIDE, late, 0)
+        lax.fori_loop(0, KUSED // KWIDE, late, 0)
         energy = lax.dot_general(gather, sq_hi[...], NT_DIMS, preferred_element_type=jnp.float32)
         energy = energy + lax.dot_general(gather, sq_lo[...], NT_DIMS, preferred_element_type=jnp.float32)
         tiles = [energy[:, a * LANES : (a + 1) * LANES] for a in range(KBLOCKS)]
-        for x in (0, 2):
+        for x in range(4):
+            own = [tile[16 * x : 16 * x + 16] for tile in (reversed(tiles) if x % 2 else tiles)]
+            if x:
+                high, low = halves(jnp.concatenate(own, axis=0))
+                place = places[x].astype(jnp.bfloat16)
+                moved = dot(high, place) + dot(low, place)
+                own = [moved[16 * a : 16 * a + 16] for a in range(KBLOCKS)]
             for a in range(KBLOCKS):
-                tile = tiles[a][16 * x : 16 * x + 16]
-                cand[x, a] = turned(tile, x) if x else tile
-        ahead = jnp.concatenate([tile[16 * x : 16 * x + 16] for x in (1, 3) for tile in reversed(tiles)], axis=0)
-        e_hi, e_lo = halves(ahead)
-        back = dot(e_hi, flip) + dot(e_lo, flip)
-        for x in (1, 3):
-            for a in range(KBLOCKS):
-                at = (x // 2 * KBLOCKS + a) * 16
-                cand[x, a] = turned(back[at : at + 16], x)
+                cand[x, a] = own[a]
 
         lane = lax.broadcasted_iota(jnp.int32, (16, LANES), 1)
 
-        for t in range(TILES):
+        def tile_at(t):
             place = t * LANES + lane
             picked = []
             for x in range(4):
@@ -444,29 +465,35 @@
             value = jnp.where(place <= 2 * quarter, picked[1], value)
             value = jnp.where(place <= quarter, picked[0], value)
             energy_out[pl.ds(t, 16, stride=ROWTILES), :] = value
-        for t in range(TILES, ROWTILES):
-            energy_out[pl.ds(t, 16, stride=ROWTILES), :] = jnp.zeros((16, LANES), jnp.float32)
 
         half, band = wave // 8, lax.rem(wave, 8)
         member = half * LEVS + lev
 
-        def rows_of(k):
-            return pl.ds(pl.multiple_of(k * ROWTILES, 8), ROWTILES)
-
-        def send_back(d, carry):
-            k = member ^ d
-            pltpu.make_async_remote_copy(
-                src_ref=energy_out.at[rows_of(k)],
-                dst_ref=got.at[rows_of(member)],
-                send_sem=back_send,
-                recv_sem=back_recv,
-                device_id=(band + 8 * (k >> 3), k & 7),
-                device_id_type=MESH,
-            ).start()
-            return carry
-
-        lax.fori_loop(1, 16, send_back, 0)
-        mine = pltpu.make_async_copy(energy_out.at[rows_of(member)], got.at[rows_of(member)], own_sem.at[0])
+        def rows_of(k, piece):
+            return pl.ds(pl.multiple_of(k * ROWTILES + piece * 16, 8), 16)
+
+        for piece in range(3):
+            for t in range(piece * 16, piece * 16 + 16):
+                if t < TILES:
+                    tile_at(t)
+                else:
+                    energy_out[pl.ds(t, 16, stride=ROWTILES), :] = jnp.zeros((16, LANES), jnp.float32)
+
+            def send_back(d, carry):
+                k = member ^ (16 - d)
+                pltpu.make_async_remote_copy(
+                    src_ref=energy_out.at[rows_of(k, piece)],
+                    dst_ref=got.at[rows_of(member, piece)],
+                    send_sem=back_send,
+                    recv_sem=back_recv,
+                    device_id=(band + 8 * (k >> 3), k & 7),
+                    device_id_type=MESH,
+                ).start()
+                return carry
+
+            lax.fori_loop(1, 16, send_back, 0)
+        whole = pl.ds(pl.multiple_of(member * ROWTILES, 8), ROWTILES)
+        mine = pltpu.make_async_copy(energy_out.at[whole], got.at[whole], own_sem.at[0])
         mine.start()
         mine.wait()
 
@@ -486,9 +513,8 @@
 
 
 def local(spectral, legendre, wave_map, row_points, brackets, lev_weight, climatology):
-    smem = pl.BlockSpec(memory_space=pltpu.SMEM)
     vmem = pl.BlockSpec(memory_space=pltpu.VMEM)
-    hbm = pl.BlockSpec(memory_space=pl.ANY)
+    hbm = pl.BlockSpec(memory_space=pltpu.HBM)
     rows = SLOTS * PER_SLOT
     f32, bf16, dma = jnp.float32, jnp.bfloat16, pltpu.SemaphoreType.DMA
     energy = pl.pallas_call(
@@ -496,16 +522,21 @@
         grid=(STEPS,),
         out_shape=jax.ShapeDtypeStruct((1, 16, ROWPAD), f32),
         in_specs=[
-            smem,
-            smem,
-            smem,
-            smem,
-            vmem,
+            hbm,
+            hbm,
+            hbm,
+            hbm,
             hbm,
             hbm,
         ],
         out_specs=vmem,
         scratch_shapes=[
+            pltpu.SMEM((M,), jnp.int32),
+            pltpu.SMEM((LEVS,), jnp.int32),
+            pltpu.SMEM((LEVS,), f32),
+            pltpu.SMEM((HALF,), jnp.int32),
+            pltpu.VMEM((M,), jnp.int32),
+            dma((5,)),
             pltpu.VMEM((BUFFERS, STEP_SLOTS, LEV_DEV * COLS, NT), bf16),
             pltpu.VMEM((BUFFERS, STEP_SLOTS, HALF, NT), bf16),
             dma((2, BUFFERS)),
@@ -547,7 +578,7 @@
             collective_id=0, has_side_effects=True, vmem_limit_bytes=58 * 1024 * 1024
         ),
         name="transform",
-    )(wave_map, brackets, lev_weight, row_points, wave_map, spectral, legendre)
+    )(wave_map, brackets, lev_weight, row_points, spectral, legendre)
     return jnp.where(energy < 0.0, 0.0, energy - climatology)
 
 

time: 56.3 us -> 55.4 us (0.984)
  Pallas kernels: 54.3 us -> 53.5 us
    pallas_call x1, Pallas kernels: 54.3 us -> 53.5 us  [local(): pl.pallas_call(kernel, grid=(STEPS,), out_shape=jax.ShapeDtypeStruct((1,...]
where the time goes in v4:
time: 55.4 us; the launch traced here: 55.3 us
  Pallas kernels  53.5 us (97%)
  other arithmetic  1.74 us (3%)
    pallas_call x1, Pallas kernels, local(): pl.pallas_call(kernel, grid=(STEPS,), out_shape=jax.ShapeDtypeStruct((1,...  53.5 us
    select_n x1, other arithmetic, local(): return jnp.where(energy < 0.0, 0.0, energy - climatology)  1.74 us

profile of v4, /device:TPU:1, one launch (start us, length us, event | category | flops | bytes accessed | tf_op | source)
XLA Modules:
  0.0 55.3 jit_solution(5674802804882779073)
XLA Ops:
  0.0 0.0 copy-start
  0.0 53.5 %transform.1 = f32[1,16,5248]{2,1,0:T(8,128)} custom-call(s32[1280]{0:T(1024)} %waves_hbm.1, s32[8]{0:T(128)} %brackets_hbm.1, f32[8]{0:T(128)} %weight_hbm.1, s32[128]{0:T(128)} %points_hbm.1, bf16[80,64,1280]{2,1,0:T(8,128)(2,1)} %spec_hbm.1, bf16[80,128,1280]{2,1,0:T(8,128)(2,1)} %leg_hbm.1), custom_call_target="tpu_custom_call" | custom-call | tf_op jit(solution)/shard_map/transform/pallas_call | solution.py:520
  53.6 0.0 copy-done
  53.6 1.7 %subtract_select_fusion = f32[1,16,5248]{2,1,0:T(8,128)} fusion(f32[1,16,5248]{2,1,0:T(8,128)} %transform.1, f32[1,16,5248]{2,1,0:T(8,128)S(1)} %copy-done), kind=kLoop, calls=%fused_computation | loop fusion | flops 251904 | bytes 1007616 | tf_op jit(solution)/shard_map/jit(_where)/select_n | solution.py:582
Async XLA Ops:
  0.0 53.6 %copy-start = (f32[1,16,5248]{2,1,0:T(8,128)S(1)}, f32[1,16,5248]{2,1,0:T(8,128)}, u32[]{:S(2)}) copy-start(f32[1,16,5248]{2,1,0:T(8,128)} %param.13) | copy-start | bytes 1007620

commit v5 on v4

--- a/solution.py
+++ b/solution.py
@@ -32,6 +32,11 @@
 PART_AT = (0, 16, 32)
 PART_SLOT = (0, WAVES * 32, WAVES * 64)
 BUFFERS = 4
+SCALE = float(2**28)
+AT_POINTS = M
+AT_BRACKETS = M + HALF
+AT_WEIGHT = AT_BRACKETS + LEVS
+SMALL = AT_WEIGHT + LEVS
 STRIDE = 37
 
 KBLOCK = 128
@@ -75,8 +80,8 @@
 
 
 def kernel(
-    waves_hbm, brackets_hbm, weight_hbm, points_hbm, spec_hbm, leg_hbm, out_ref,
-    waves_ref, brackets_ref, weight_ref, points_ref, orders_ref, small_sem, spec_ref, leg_ref, load_sem, mixed, first, other, send, recv, coef, sign, re_hi, re_lo, im_hi, im_lo,
+    small_hbm, spec_hbm, leg_hbm, out_ref,
+    small_ref, orders_ref, small_sem, spec_ref, leg_ref, load_sem, mixed, first, other, send, recv, coef, sign, re_hi, re_lo, im_hi, im_lo,
     fine_c, fine_s, coarse_c, coarse_s, cos_hi, cos_lo, sin_hi, sin_lo, acc, sq_hi, sq_lo, cand, energy_out, got,
     near_send, near_recv, far_send, far_recv, own_sem, back_send, back_recv, ready,
 ):
@@ -97,11 +102,8 @@
         pltpu.make_async_copy(source, target, small_sem.at[i])
         for i, (source, target) in enumerate(
             (
-                (brackets_hbm, brackets_ref),
-                (weight_hbm, weight_ref),
-                (waves_hbm, waves_ref),
-                (points_hbm, points_ref),
-                (waves_hbm, orders_ref),
+                (small_hbm, small_ref),
+                (small_hbm, orders_ref),
             )
         )
     ]
@@ -135,16 +137,16 @@
         for small in smalls:
             small.wait()
 
-    lower = brackets_ref[lev] - lev * LEV_DEV
-    weight = weight_ref[lev]
+    lower = small_ref[AT_BRACKETS + lev] - lev * LEV_DEV
+    weight = small_ref[AT_WEIGHT + lev].astype(jnp.float32) * (1.0 / SCALE)
     gain = jnp.where(lower == LEV_DEV - 1, 1.0 - weight, 0.0)
     odd = (lev & 1) == 1
     even = (lev & 1) == 0
     wide = even & (lev > 0)
     narrow = odd | (lev == 0)
     prior = jnp.maximum(lev - 1, 0)
-    prior_last = (brackets_ref[prior] == prior * LEV_DEV + LEV_DEV - 1) & (lev > 0)
-    prior_gain = jnp.where(prior_last, 1.0 - weight_ref[prior], 0.0)
+    prior_last = (small_ref[AT_BRACKETS + prior] == prior * LEV_DEV + LEV_DEV - 1) & (lev > 0)
+    prior_gain = jnp.where(prior_last, 1.0 - small_ref[AT_WEIGHT + prior].astype(jnp.float32) * (1.0 / SCALE), 0.0)
     level_weight = [
         jnp.where(lower == v, weight, 0.0) + jnp.where(lower + 1 == v, 1.0 - weight, 0.0) for v in range(LEV_DEV)
     ]
@@ -283,7 +285,7 @@
     held_at = lax.rem(step, BUFFERS)
     degree = lax.broadcasted_iota(jnp.int32, (1, NT), 1)
     for i in range(STEP_SLOTS):
-        order = waves_ref[wave * SLOTS + step * STEP_SLOTS + i]
+        order = small_ref[wave * SLOTS + step * STEP_SLOTS + i]
         kept = jnp.where(degree >= order, 1.0, 0.0)
         signed = kept * (1 - 2 * ((degree + order) & 1)).astype(jnp.float32)
         kept, signed = kept.astype(jnp.bfloat16), signed.astype(jnp.bfloat16)
@@ -309,9 +311,9 @@
         assemble_part(2)
         push(2)
 
-        count = points_ref[pair_of(wave, lev)]
+        count = small_ref[AT_POINTS + pair_of(wave, lev)]
         points = count.astype(jnp.float32)
-        natural = orders_ref[...].reshape(1, M).astype(jnp.float32)
+        natural = orders_ref[...][:M].reshape(1, M).astype(jnp.float32)
         pieces = []
         for begin, slots, _ in PARTS:
             pieces += [natural[:, w * SLOTS + begin : w * SLOTS + begin + slots] for w in range(WAVES)]
@@ -514,6 +516,7 @@
 
 def local(spectral, legendre, wave_map, row_points, brackets, lev_weight, climatology):
     vmem = pl.BlockSpec(memory_space=pltpu.VMEM)
+    small = jnp.concatenate([wave_map, row_points, brackets, (lev_weight * SCALE).astype(jnp.int32)])
     hbm = pl.BlockSpec(memory_space=pltpu.HBM)
     rows = SLOTS * PER_SLOT
     f32, bf16, dma = jnp.float32, jnp.bfloat16, pltpu.SemaphoreType.DMA
@@ -525,18 +528,12 @@
             hbm,
             hbm,
             hbm,
-            hbm,
-            hbm,
-            hbm,
         ],
         out_specs=vmem,
         scratch_shapes=[
-            pltpu.SMEM((M,), jnp.int32),
-            pltpu.SMEM((LEVS,), jnp.int32),
-            pltpu.SMEM((LEVS,), f32),
-            pltpu.SMEM((HALF,), jnp.int32),
-            pltpu.VMEM((M,), jnp.int32),
-            dma((5,)),
+            pltpu.SMEM((SMALL,), jnp.int32),
+            pltpu.VMEM((SMALL,), jnp.int32),
+            dma((2,)),
             pltpu.VMEM((BUFFERS, STEP_SLOTS, LEV_DEV * COLS, NT), bf16),
             pltpu.VMEM((BUFFERS, STEP_SLOTS, HALF, NT), bf16),
             dma((2, BUFFERS)),
@@ -575,10 +572,10 @@
             pltpu.SemaphoreType.REGULAR,
         ],
         compiler_params=pltpu.CompilerParams(
-            collective_id=0, has_side_effects=True, vmem_limit_bytes=58 * 1024 * 1024
+            collective_id=0, has_side_effects=True, vmem_limit_bytes=52 * 1024 * 1024
         ),
         name="transform",
-    )(wave_map, brackets, lev_weight, row_points, spectral, legendre)
+    )(small, spectral, legendre)
     return jnp.where(energy < 0.0, 0.0, energy - climatology)
 
 

time: 55.4 us -> 53 us (0.957)
  Pallas kernels: 53.5 us -> 50.6 us
  local copies, waits for them, and re-layouts: 0.01 us -> 0.77 us
    pallas_call x1, Pallas kernels: 53.5 us -> 50.6 us  [local(): pl.pallas_call(kernel, grid=(STEPS,), out_shape=jax.ShapeDtypeStruct((1,...]
    select_n x1, other arithmetic: 1.74 us -> 0.77 us  [local(): return jnp.where(energy < 0.0, 0.0, energy - climatology)]
    concatenate x0 -> x1, local copies, waits for them, and re-layouts: none -> 0.77 us  [local(): jnp.concatenate([wave_map, row_points, brackets, (lev_weight * SCALE).ast...]
    convert_element_type x0 -> x1, other arithmetic: none -> 0.71 us  [local(): (lev_weight * SCALE).astype(jnp.int32)]
where the time goes in v5:
time: 53 us; the launch traced here: 52.9 us
  Pallas kernels  50.6 us (95%)
  other arithmetic  1.47 us (3%)
  local copies, waits for them, and re-layouts  0.77 us (1%)
    pallas_call x1, Pallas kernels, local(): pl.pallas_call(kernel, grid=(STEPS,), out_shape=jax.ShapeDtypeStruct((1,...  50.6 us

profile of v5, /device:TPU:1, one launch (start us, length us, event | category | flops | bytes accessed | tf_op | source)
XLA Modules:
  0.0 52.9 jit_solution(5489652803588583632)
XLA Ops:
  0.0 0.0 copy-start
  0.0 0.7 %multiply_convert_fusion = s32[8]{0:T(128)S(1)} fusion(f32[8]{0:T(128)} %param.12), kind=kLoop, calls=%fused_computation.1 | loop fusion | flops 16 | bytes 64 | tf_op jit(solution)/shard_map/convert_element_type | solution.py:519
  0.7 0.8 %concatenate.3.small_hbm = s32[1424]{0:T(1024)S(1)} concatenate(s32[1280]{0:T(1024)} %param.9, s32[128]{0:T(128)} %param.10, s32[8]{0:T(128)} %param.11, s32[8]{0:T(128)S(1)} %multiply_convert_fusion), dimensions={0} | concatenate | bytes 11392 | tf_op jit(solution)/shard_map/concatenate | solution.py:519
  1.5 50.6 %transform.1 = f32[1,16,5248]{2,1,0:T(8,128)S(1)} custom-call(s32[1424]{0:T(1024)S(1)} %concatenate.3.small_hbm, bf16[80,64,1280]{2,1,0:T(8,128)(2,1)} %spec_hbm.1, bf16[80,128,1280]{2,1,0:T(8,128)(2,1)} %leg_hbm.1), custom_call_target="tpu_custom_call" | custom-call | tf_op jit(solution)/shard_map/transform/pallas_call | solution.py:523
  52.1 0.0 copy-done
  52.1 0.8 %subtract_select_fusion = f32[1,16,5248]{2,1,0:T(8,128)} fusion(f32[1,16,5248]{2,1,0:T(8,128)S(1)} %transform.1, f32[1,16,5248]{2,1,0:T(8,128)S(1)} %copy-done), kind=kLoop, calls=%fused_computation | loop fusion | flops 251904 | bytes 1007616 | tf_op jit(solution)/shard_map/jit(_where)/select_n | solution.py:579
Async XLA Ops:
  0.0 52.1 %copy-start = (f32[1,16,5248]{2,1,0:T(8,128)S(1)}, f32[1,16,5248]{2,1,0:T(8,128)}, u32[]{:S(2)}) copy-start(f32[1,16,5248]{2,1,0:T(8,128)} %param.13) | copy-start | bytes 1007620
